TPU v7x, 32 devices: a whole 2x2x4 slice. The times are simulated.
32 devices in a mesh: dp: 4 (over y, core), tensor: 8 (over z, x).
Axes of the slice: x: 2, y: 2, z: 4, core: 2. Of those that a mesh axis runs over, the one named last changes fastest.
Arguments:
- tokens: bfloat16 [8192, 1024], P(('dp', 'tensor')), may hold values from -6 to 6
- segment_ids: int32 [4, 2048], P('dp'), may hold values from 0 to 3, never falling along the last dimension, each value on 1 to 1024 neighbouring positions
- cotangent: bfloat16 [8192, 1024], P(('dp', 'tensor')), may hold values from -6 to 6
- attn_gain: float32 [1024], replicated, may hold values from 0.5 to 1.5
- query_weight: bfloat16 [1024, 1024], P('dp', 'tensor'), may hold values from -0.1875 to 0.1875
- key_weight: bfloat16 [1024, 512], P('dp', 'tensor'), may hold values from -0.1875 to 0.1875
- value_weight: bfloat16 [1024, 512], P('dp', 'tensor'), may hold values from -0.1875 to 0.1875
- output_weight: bfloat16 [1024, 1024], P('tensor', 'dp'), may hold values from -0.75 to 0.75
- query_gain: float32 [64], replicated, may hold values from 0.5 to 1.5
- key_gain: float32 [64], replicated, may hold values from 0.5 to 1.5
- ffn_gain: float32 [1024], replicated, may hold values from 0.5 to 1.5
- gate_weight: bfloat16 [1024, 4608], P('dp', 'tensor'), may hold values from -0.1875 to 0.1875
- up_weight: bfloat16 [1024, 4608], P('dp', 'tensor'), may hold values from -0.1875 to 0.1875
- down_weight: bfloat16 [4608, 1024], P('tensor', 'dp'), may hold values from -0.09375 to 0.09375
Outputs:
- block_out: bfloat16 [8192, 1024], P(('dp', 'tensor'))
- input_grad: bfloat16 [8192, 1024], P(('dp', 'tensor'))
- attn_gain_grad: float32 [1024], replicated
- query_grad: float32 [1024, 1024], P('dp', 'tensor')
- key_grad: float32 [1024, 512], P('dp', 'tensor')
- value_grad: float32 [1024, 512], P('dp', 'tensor')
- output_grad: float32 [1024, 1024], P('tensor', 'dp')
- query_gain_grad: float32 [64], replicated
- key_gain_grad: float32 [64], replicated
- ffn_gain_grad: float32 [1024], replicated
- gate_grad: float32 [1024, 4608], P('dp', 'tensor')
- up_grad: float32 [1024, 4608], P('dp', 'tensor')
- down_grad: float32 [4608, 1024], P('tensor', 'dp')
Inputs may be any that keep to these rules, and one draw needn't show every extreme that they name: `segment_ids`: in each row the numbers never fall; every run of one number covers 1 to 1024 positions, and some run covers exactly 1024.
All inputs are finite; a program needn't handle non-finite values.
Results may differ from a plain program's by a relative error of at most 0.022.
Values may be sent and summed in bfloat16 or wider, within the bound.
No kernel may reach another device: no remote copies, remote signals or barrier semaphores. Data moves between devices by JAX's collectives and lax.ppermute only.
A program may use at most 128 MiB of HBM per device.

v0:
```python
import functools

import jax
import jax.numpy as jnp
from jax import lax
from jax.experimental import pallas as pl
from jax.experimental.pallas import tpu as pltpu
from jax.sharding import Mesh
from jax.sharding import PartitionSpec as P

EPSILON = 1e-05
ROPE_BASE = 1000000.0
BLOCK = 256
F32 = jnp.float32
BF16 = jnp.bfloat16
VMEM_LIMIT = 40 * 1024 * 1024
NO_COST = pl.CostEstimate(flops=0, bytes_accessed=0, transcendentals=0)

NEAR = ("zl", "x")
TENSOR = ("zh", "zl", "x")


def nn(a, b):
    return lax.dot_general(a, b, (((1,), (0,)), ((), ())), preferred_element_type=F32)


def nt(a, b):
    return lax.dot_general(a, b, (((1,), (1,)), ((), ())), preferred_element_type=F32)


def tn(a, b):
    return lax.dot_general(a, b, (((0,), (0,)), ((), ())), preferred_element_type=F32)


def params(**more):
    return pltpu.CompilerParams(vmem_limit_bytes=VMEM_LIMIT, **more)


def swap(v, axes, bit):
    size = lax.axis_size(axes)
    return lax.ppermute(v, axes, [(i, i ^ bit) for i in range(size)])


def quads(v):
    return jnp.split(v, 4, axis=-1)


def own_order(v, y, c):
    runs = lax.axis_size("r")
    if runs > 1:
        lead = v.shape[:-1]
        v = jnp.moveaxis(v.reshape(lead + (runs, 4, -1)), -3, -2).reshape(lead + (-1,))
    return exchange(v, y, c)


def exchange(v, y, c):
    a = quads(v)
    a = [jnp.where(c == 0, a[e], a[e ^ 1]) for e in range(4)]
    return jnp.concatenate([jnp.where(y == 0, a[e], a[e ^ 2]) for e in range(4)], axis=-1)


def arrays_order(v, y, c):
    v = exchange(v, y, c)
    runs = lax.axis_size("r")
    if runs > 1:
        lead = v.shape[:-1]
        v = jnp.moveaxis(v.reshape(lead + (4, runs, -1)), -2, -3).reshape(lead + (-1,))
    return v


def gather_runs(v):
    return lax.all_gather(v, "r", axis=v.ndim - 1, tiled=True) if lax.axis_size("r") > 1 else v


def scatter_runs(v):
    if lax.axis_size("r") == 1:
        return v
    return lax.psum_scatter(
        v.astype(BF16), "r", scatter_dimension=v.ndim - 1, tiled=True
    ).astype(F32)


def total_of(v):
    if lax.axis_size("r") > 1:
        v = lax.psum(v, "r")
    axes = ("y", "c") + TENSOR
    every = jnp.broadcast_to(v[None], (lax.axis_size(axes),) + v.shape)
    return jnp.sum(lax.all_to_all(every, axes, 0, 0, tiled=True), axis=0)


def after(later, *done):
    later, done = lax.optimization_barrier((later, done))
    return (later,) + tuple(done)


def add_swapped(keep, send, axes, bit):
    return keep.astype(F32) + swap(send, axes, bit).astype(F32)


def halves(v):
    return jnp.split(v, 2, axis=-1)


def lanes_of(shape):
    return lax.broadcasted_iota(jnp.int32, shape, len(shape) - 1)


def head_sums(v, head):
    width = v.shape[-1]
    row = lax.broadcasted_iota(jnp.int32, (width, width), 0) // head
    col = lax.broadcasted_iota(jnp.int32, (width, width), 1) // head
    ones = jnp.where(row == col, 1.0, 0.0).astype(BF16)
    high = v.astype(BF16)
    return nn(high, ones) + nn((v - high.astype(F32)).astype(BF16), ones)


def swap_halves(v, head):
    width, half = v.shape[-1], head // 2
    low = (lanes_of(v.shape) % head) < half
    return jnp.where(low, pltpu.roll(v, width - half, 1), pltpu.roll(v, half, 1))


def rope_prep(v, gain, cosine, sine, head):
    factor = lax.rsqrt(head_sums(v * v, head) * (1.0 / head) + EPSILON)
    n = v * factor * gain
    return n * cosine + swap_halves(n, head) * sine


def project_qkv(xa, w, slot, n):
    cols = w[0].shape[-1]
    return sum(nt(xa[:, e * cols : (e + 1) * cols], piece(w, slot, e)[:n]) for e in range(4))


def piece(w, slot, e):
    return w[e % 2][(e // 2) * 2 + slot]


def qkv_kernel(head, slot, *refs):
    xa, w = refs[:4], refs[4:6]
    cosine, sine, q_gain, k_gain, low = refs[6:]
    n = low.shape[-1]
    width = 2 * head
    for i in range(4):
        proj = project_qkv(xa[i], w, slot, n)
        q = rope_prep(proj[:, :width], q_gain[...], cosine[i], sine[i], head)
        kv = proj[:, width:]
        k = rope_prep(kv, k_gain[...], cosine[i], sine[i], head)
        low[i, :, :width] = q.astype(BF16)
        low[i, :, width:] = jnp.where(lanes_of(kv.shape) < head, k, kv).astype(BF16)


def qkv_call(xa, w, slot, cosine, sine, q_gain, k_gain, head):
    rows, n = xa[0].shape[0], w[1].shape[1]
    return pl.pallas_call(
        functools.partial(qkv_kernel, head, slot),
        out_shape=jax.ShapeDtypeStruct((4, rows, n), BF16),
        compiler_params=params(),
        cost_estimate=NO_COST,
        name="qkv",
    )(*xa, *w, cosine, sine, q_gain, k_gain)


def stack_heads(v, head, scale=None):
    out = jnp.concatenate([v[:, :head], v[:, head : 2 * head]], axis=0)
    return out if scale is None else (out.astype(F32) * scale).astype(BF16)


def unstack(v_t):
    rows = v_t.shape[1] // 2
    return jnp.concatenate([v_t[:, :rows], v_t[:, rows:]], axis=0).T


def attend_kernel(head, first, at, *refs):
    parts = refs[:2]
    start, context, log_total, qkv, turned = refs[2:]
    b = pl.program_id(0)
    width = 2 * head

    @pl.when(b == 0)
    def _():
        done = 0
        for part in parts:
            for i in range(part.shape[0]):
                place = pl.multiple_of(at[done] * BLOCK, BLOCK)
                qkv[pl.ds(place, BLOCK), :] = part[i]
                done += 1
        kv_t = qkv[:, width:].astype(F32).T
        row = lax.broadcasted_iota(jnp.int32, kv_t.shape, 0)
        turned[...] = jnp.where(row < head, 1.0, kv_t).astype(BF16)

    q2 = stack_heads(qkv[pl.ds(b * BLOCK, BLOCK), :width], head, head**-0.5)
    begin = start[0]
    key = lax.broadcasted_iota(jnp.int32, (BLOCK, 2 * BLOCK), 0)

    def block(j, acc, diagonal):
        s = nt(qkv[pl.ds(j * BLOCK, BLOCK), width : width + head], q2)
        allowed = key >= begin - j * BLOCK
        if diagonal:
            row = lanes_of((BLOCK, 2 * BLOCK)) % BLOCK
            allowed = allowed & (key <= row)
        p = jnp.where(allowed, jnp.exp(s), 0.0)
        return acc + nn(turned[:, pl.ds(j * BLOCK, BLOCK)], p.astype(BF16))

    acc = jnp.zeros((width, 2 * BLOCK), F32)
    acc = lax.fori_loop(first[b], b, lambda j, acc: block(j, acc, False), acc)
    acc = block(b, acc, True)
    total = acc[:1]
    context[...] = unstack(acc[head:] / total).astype(BF16)
    log_total[0] = jnp.log(total)


def attend_call(first, at, parts, start, head):
    n = parts[0].shape[-1]
    rows = sum(v.shape[0] for v in parts) * BLOCK
    blocks = rows // BLOCK
    whole = lambda shape: pl.BlockSpec(shape, lambda b, first, at: (0,) * len(shape))
    return pl.pallas_call(
        functools.partial(attend_kernel, head),
        grid_spec=pltpu.PrefetchScalarGridSpec(
            num_scalar_prefetch=2,
            grid=(blocks,),
            in_specs=[whole(v.shape) for v in parts]
            + [pl.BlockSpec((1, 1, 2 * BLOCK), lambda b, first, at: (b, 0, 0))],
            out_specs=[
                pl.BlockSpec((BLOCK, 2 * head), lambda b, first, at: (b, 0)),
                pl.BlockSpec((1, 1, 2 * BLOCK), lambda b, first, at: (b, 0, 0)),
                whole((rows, n)),
            ],
            scratch_shapes=[pltpu.VMEM((2 * head, rows), BF16)],
        ),
        out_shape=[
            jax.ShapeDtypeStruct((rows, 2 * head), BF16),
            jax.ShapeDtypeStruct((blocks, 1, 2 * BLOCK), F32),
            jax.ShapeDtypeStruct((rows, n), BF16),
        ],
        compiler_params=params(),
        cost_estimate=NO_COST,
        name="attend",
    )(first, at, *parts, start)


def attend_back_kernel(
    head, first, to, qkv, context, d_context, start, log_total, out, turned, d_key, d_value
):
    b = pl.program_id(0)
    width = 2 * head

    @pl.when(b == 0)
    def _():
        turned[...] = qkv[:, width:].astype(F32).T.astype(BF16)
        d_key[...] = jnp.zeros_like(d_key)
        d_value[...] = jnp.zeros_like(d_value)

    scale = head**-0.5
    q2 = stack_heads(qkv[pl.ds(b * BLOCK, BLOCK), :width], head, scale)
    g = d_context[...]
    g2 = stack_heads(g, head)
    begin = start[0]
    log_sum = log_total[0]
    picks = jnp.where(
        lanes_of((8, width)) // head == lax.broadcasted_iota(jnp.int32, (8, width), 0), 1.0, 0.0
    ).astype(F32)
    delta = lax.dot_general(
        picks,
        g.astype(F32) * context[...].astype(F32),
        (((1,), (1,)), ((), ())),
        preferred_element_type=F32,
        precision=lax.Precision.HIGHEST,
    )
    delta = jnp.concatenate([delta[0:1], delta[1:2]], axis=1)
    key = lax.broadcasted_iota(jnp.int32, (BLOCK, 2 * BLOCK), 0)

    def block(j, acc, diagonal):
        at = pl.ds(j * BLOCK, BLOCK)
        s = nt(qkv[at, width : width + head], q2)
        allowed = key >= begin - j * BLOCK
        if diagonal:
            row = lanes_of((BLOCK, 2 * BLOCK)) % BLOCK
            allowed = allowed & (key <= row)
        p = jnp.where(allowed, jnp.exp(s - log_sum), 0.0)
        d_p = nt(qkv[at, width + head :], g2)
        d_s = (p * (d_p - delta)).astype(BF16)
        d_value[at, :] += nn(p.astype(BF16), g2)
        d_key[at, :] += nn(d_s, q2)
        return acc + nn(turned[:, at], d_s)

    acc = jnp.zeros((width, 2 * BLOCK), F32)
    acc = lax.fori_loop(first[b], b, lambda j, acc: block(j, acc, False), acc)
    acc = block(b, acc, True)
    out[to[b], :, :width] = (unstack(acc[:head]) * scale).astype(BF16)

    @pl.when(b == pl.num_programs(0) - 1)
    def _():
        for j in range(out.shape[0]):
            at = pl.ds(j * BLOCK, BLOCK)
            out[to[j], :, width:] = jnp.concatenate([d_key[at, :], d_value[at, :]], axis=1).astype(
                BF16
            )


def attend_back_call(first, to, qkv, context, d_context, start, log_total, head):
    rows, n = qkv.shape
    blocks = rows // BLOCK
    per_block = pl.BlockSpec((BLOCK, 2 * head), lambda b, first, to: (b, 0))
    per_row = pl.BlockSpec((1, 1, 2 * BLOCK), lambda b, first, to: (b, 0, 0))
    return pl.pallas_call(
        functools.partial(attend_back_kernel, head),
        grid_spec=pltpu.PrefetchScalarGridSpec(
            num_scalar_prefetch=2,
            grid=(blocks,),
            in_specs=[
                pl.BlockSpec((rows, n), lambda b, first, to: (0, 0)),
                per_block,
                per_block,
                per_row,
                per_row,
            ],
            out_specs=pl.BlockSpec((blocks, BLOCK, n), lambda b, first, to: (0, 0, 0)),
            scratch_shapes=[
                pltpu.VMEM((2 * head, rows), BF16),
                pltpu.VMEM((rows, head), F32),
                pltpu.VMEM((rows, head), F32),
            ],
        ),
        out_shape=jax.ShapeDtypeStruct((blocks, BLOCK, n), BF16),
        compiler_params=params(),
        cost_estimate=NO_COST,
        name="attend_back",
    )(first, to, qkv, context, d_context, start, log_total)


def joined(context, at, q):
    return jnp.concatenate([context[at[q]], context[at[4 + q]]], axis=1)


def piece_of(w, q, e, cols):
    v = w[e % 2][2 * q : 2 * q + 2, :, (e // 2) * cols : (e // 2 + 1) * cols]
    return v.reshape(-1, cols)


def project_kernel(at, context, w_near, w_far, x, gain, hidden, normed):
    cols = w_near.shape[-1] // 2
    left = [joined(context, at, q) for q in range(4)]
    for e in range(4):
        to = slice(e * cols, (e + 1) * cols)
        hidden[:, to] = x[:, to] + sum(
            nn(left[q], piece_of((w_near, w_far), q, e, cols)) for q in range(4)
        )
    h = hidden[...]
    factor = lax.rsqrt(jnp.mean(h * h, axis=-1, keepdims=True) + EPSILON)
    normed[...] = (h * factor * gain[...]).astype(BF16)


def in_vmem(count):
    return [pl.BlockSpec(memory_space=pltpu.VMEM)] * count


def project_call(at, context, w, x, gain):
    rows, d = x.shape
    return pl.pallas_call(
        project_kernel,
        in_specs=[pl.BlockSpec(memory_space=pltpu.SMEM)] + in_vmem(5),
        out_shape=[jax.ShapeDtypeStruct((rows, d), F32), jax.ShapeDtypeStruct((rows, d), BF16)],
        compiler_params=params(),
        cost_estimate=NO_COST,
        name="project",
    )(at, context, w[0], w[1], x, gain)


def project_back_kernel(
    at, context, w_near, w_far, hidden, gain, dy, p0, p1, p2, p3, d_context, keep, send, d_hidden, part
):
    cols = w_near.shape[-1] // 2
    n = context.shape[-1]
    h = hidden[...]
    g = (p0[...].astype(F32) + p1[...].astype(F32)) + (p2[...].astype(F32) + p3[...].astype(F32))
    factor = lax.rsqrt(jnp.mean(h * h, axis=-1, keepdims=True) + EPSILON)
    part[...] = jnp.sum(g * h * factor, axis=0, keepdims=True)
    u = gain[...] * g
    mean = jnp.mean(u * h, axis=-1, keepdims=True)
    out = dy[...].astype(F32) + (factor * u - h * (factor * factor * factor * mean))
    d_hidden[...] = out
    low = out.astype(BF16)
    for q in range(4):
        both = sum(
            nt(low[:, e * cols : (e + 1) * cols], piece_of((w_near, w_far), q, e, cols))
            for e in range(4)
        ).astype(BF16)
        d_context[at[q]] = both[:, :n]
        d_context[at[4 + q]] = both[:, n:]
    for q in range(4):
        grad = tn(joined(context, at, q), low).astype(BF16)
        for s in (0, 1):
            rows = slice(s * n, (s + 1) * n)
            keep[2 * q + s, :, :cols] = grad[rows, :cols]
            send[2 * q + s, :, :cols] = grad[rows, cols : 2 * cols]
            keep[2 * q + s, :, cols:] = grad[rows, 2 * cols : 3 * cols]
            send[2 * q + s, :, cols:] = grad[rows, 3 * cols :]


def project_back_call(at, context, w, hidden, gain, dy, parts):
    rows, d = hidden.shape
    grad = jax.ShapeDtypeStruct(w[0].shape, BF16)
    return pl.pallas_call(
        project_back_kernel,
        in_specs=[pl.BlockSpec(memory_space=pltpu.SMEM)] + in_vmem(10),
        out_shape=[
            jax.ShapeDtypeStruct(context.shape, BF16),
            grad,
            grad,
            jax.ShapeDtypeStruct((rows, d), F32),
            jax.ShapeDtypeStruct((1, d), F32),
        ],
        compiler_params=params(),
        cost_estimate=NO_COST,
        name="project_back",
    )(at, context, w[0], w[1], hidden, gain, dy, *parts)


def qkv_back_kernel(head, *refs):
    grads, xa, w = refs[:2], refs[2:6], refs[6:8]
    cosine, sine, q_gain, k_gain, a_gain = refs[8:13]
    d_xa, (keep, send, parts, a_part) = refs[13:17], refs[17:]
    n = keep.shape[1]
    width = 2 * head
    cols = w[0].shape[-1]

    def back(g, v, gain, i):
        e = g * cosine[i] - swap_halves(g, head) * sine[i]
        m = lax.rsqrt(head_sums(v * v, head) * (1.0 / head) + EPSILON)
        u = gain * e
        mean = head_sums(u * v, head) * (1.0 / head)
        return m * u - v * (m * m * m * mean), jnp.sum(e * v * m, axis=0, keepdims=True)

    lows = []
    q_sum = k_sum = 0.0
    for slot in (0, 1):
        for i in range(4):
            v, g = project_qkv(xa[i], w, slot, n), grads[slot][i].astype(F32)
            d_q, part = back(g[:, :width], v[:, :width], q_gain[...], i)
            q_sum += part
            d_k, part = back(g[:, width:], v[:, width:], k_gain[...], i)
            k_sum += part
            d_kv = jnp.where(lanes_of(d_k.shape) < head, d_k, g[:, width:])
            lows.append(jnp.concatenate([d_q, d_kv], axis=1).astype(BF16))
    for e in range(4):
        at = slice(e * cols, (e + 1) * cols)
        to = slice((e // 2) * cols, (e // 2 + 1) * cols)
        total = 0.0
        for i in range(4):
            here = nn(lows[i], piece(w, 0, e)[:n]) + nn(lows[4 + i], piece(w, 1, e)[:n])
            d_xa[i][:, at] = here.astype(BF16)
            total += jnp.sum(here * xa[i][:, at].astype(F32), axis=0, keepdims=True)
        a_part[:, at] = total / a_gain[:, at]
        for slot in (0, 1):
            here = sum(tn(lows[slot * 4 + i], xa[i][:, at]) for i in range(4))
            (keep, send)[e % 2][slot, :, to] = here.astype(BF16)
    parts[0:1] = q_sum
    parts[1:2] = k_sum


def qkv_back_call(grads, xa, w, cosine, sine, gains, head):
    rows, d = xa[0].shape
    n = w[1].shape[1]
    half = jax.ShapeDtypeStruct((2, n, d // 2), BF16)
    return pl.pallas_call(
        functools.partial(qkv_back_kernel, head),
        out_shape=[jax.ShapeDtypeStruct((rows, d), BF16)] * 4
        + [half, half]
        + [jax.ShapeDtypeStruct((2, 2 * head), F32), jax.ShapeDtypeStruct((1, d), F32)],
        compiler_params=params(),
        cost_estimate=NO_COST,
        name="qkv_back",
    )(*grads, *xa, *w, cosine, sine, *gains)


def ffn_kernel(count, *refs):
    xf, dy, w = refs[:count], refs[count : 2 * count], refs[2 * count : 2 * count + 16]
    refs = refs[2 * count + 16 :]
    cols = w[0].shape[-1]

    def piece(slot, e, which):
        return w[e][which] if slot == 0 else w[4 + 4 * which + e][...]

    def wide(v, slot, which):
        return sum(nt(v[:, e * cols : (e + 1) * cols], piece(slot, e, which)) for e in range(4))

    for i in range(count):
        acts, out, d_xf = refs[3 * i : 3 * i + 3]
        for slot in (0, 1):
            gate, up = wide(xf[i], slot, 0), wide(xf[i], slot, 1)
            d_act = wide(dy[i], slot, 2).astype(BF16).astype(F32)
            sig = 1.0 / (1.0 + jnp.exp(-gate))
            silu = gate * sig
            acts[2, slot] = (silu * up).astype(BF16)
            acts[0, slot] = (d_act * up * (sig * (1.0 + gate * (1.0 - sig)))).astype(BF16)
            acts[1, slot] = (d_act * silu).astype(BF16)
        for e in range(4):
            at = slice(e * cols, (e + 1) * cols)
            d_xf[:, at] = sum(
                nn(acts[k, slot], piece(slot, e, k)) for slot in (0, 1) for k in (0, 1)
            ).astype(BF16)
        for e in range(4):
            at = slice(e * cols, (e + 1) * cols)
            out[:, at] = sum(nn(acts[2, slot], piece(slot, e, 2)) for slot in (0, 1)).astype(BF16)


def ffn_call(xf, dy, w):
    count, (rows, d) = len(xf), xf[0].shape
    units = w[0].shape[1]
    tokens = jax.ShapeDtypeStruct((rows, d), BF16)
    return pl.pallas_call(
        functools.partial(ffn_kernel, count),
        out_shape=[jax.ShapeDtypeStruct((3, 2, rows, units), BF16), tokens, tokens] * count,
        compiler_params=params(),
        cost_estimate=NO_COST,
        name="ffn",
    )(*xf, *dy, *w)


def ffn_grad_kernel(*refs):
    acts, xf, dy = refs[:4], refs[4:8], refs[8:12]
    keep, send = refs[12:]
    cols = keep.shape[-1] // 2

    def write(right):
        for e in range(4):
            at = slice(e * cols, (e + 1) * cols)
            here = sum(tn(acts[b][0, 0], right[b][:, at]) for b in range(4)).astype(BF16)
            to = slice((e // 2) * cols, (e // 2 + 1) * cols)
            (keep, send)[e % 2][0, :, to] = here

    pl.when(pl.program_id(0) < 2)(lambda: write(xf))
    pl.when(pl.program_id(0) == 2)(lambda: write(dy))


def ffn_grad_call(acts, xf, dy, slot):
    three, _, rows, units = acts[0].shape
    d = xf[0].shape[1]
    by_kind = pl.BlockSpec((1, 1, rows, units), lambda k: (k, slot, 0, 0))
    half = pl.BlockSpec((1, units, d // 2), lambda k: (k, 0, 0))
    out = jax.ShapeDtypeStruct((three, units, d // 2), BF16)
    return pl.pallas_call(
        ffn_grad_kernel,
        grid=(three,),
        in_specs=[by_kind] * 4 + [pl.BlockSpec((rows, d), lambda k: (0, 0))] * 8,
        out_specs=[half, half],
        out_shape=[out, out],
        compiler_params=params(),
        cost_estimate=NO_COST,
        name="ffn_grad",
    )(*acts, *xf, *dy)


def norm_factor(v):
    return lax.rsqrt(jnp.mean(v * v, axis=-1, keepdims=True) + EPSILON)


def norm_back(v, factor, gain, grad):
    u = gain * grad
    part = jnp.sum(grad * v * factor, axis=0)
    mean = jnp.mean(u * v, axis=-1, keepdims=True)
    return factor * u - v * (factor * factor * factor * mean), part


def per_device(
    tokens,
    segment_ids,
    cotangent,
    attn_gain,
    query_weight,
    key_weight,
    value_weight,
    output_weight,
    query_gain,
    key_gain,
    ffn_gain,
    gate_weight,
    up_weight,
    down_weight,
):
    y, c, zh = lax.axis_index("y"), lax.axis_index("c"), lax.axis_index("zh")
    near = lax.axis_index(NEAR)
    head = query_gain.shape[0]
    rows = tokens.shape[0]
    nq, nk = query_weight.shape[1], key_weight.shape[1]
    n = nq + 2 * nk

    x = own_order(tokens, y, c).astype(F32)
    gain_a = own_order(attn_gain[None], y, c)
    gain_f = own_order(ffn_gain[None], y, c)
    gain_q = jnp.concatenate([query_gain, query_gain])[None]
    gain_k = jnp.concatenate([key_gain, key_gain])[None]
    x_factor = norm_factor(x)
    xa = (x * x_factor * gain_a).astype(BF16)
    shard = gather_runs(
        jnp.concatenate([query_weight.T, key_weight.T, value_weight.T, output_weight], axis=0)
    )
    ffn_own = gather_runs(jnp.stack([gate_weight.T, up_weight.T, down_weight]))
    xa_near = [xa, swap(xa, NEAR, 1), swap(xa, NEAR, 2)]
    heads = [shard, swap(shard, "zh", 1), swap(shard, "y", 1), swap(shard, ("y", "zh"), 3)]
    gate_far = swap(ffn_own[0], "zh", 1)
    (xa_near, ffn_own), gate_far, *heads = after((xa_near, ffn_own), gate_far, *heads)
    xa_near.append(swap(xa_near[2], NEAR, 1))
    heads = jnp.stack(heads)
    qkv_w = (heads, swap(heads[:, :n], "c", 1))
    up_far = swap(ffn_own[1], "zh", 1)
    (ffn_own, xa_near, gate_far), qkv_w, up_far = after((ffn_own, xa_near, gate_far), qkv_w, up_far)

    segment = segment_ids[0]
    total_rows = segment.shape[0]
    index = jnp.arange(total_rows, dtype=jnp.int32)
    opens = jnp.concatenate([jnp.ones((1,), dtype=jnp.bool_), segment[1:] != segment[:-1]])
    begin = lax.cummax(jnp.where(opens, index, 0), axis=0)
    blocks = total_rows // BLOCK
    first = begin[::BLOCK] // BLOCK
    by_block = begin.reshape(blocks, 1, BLOCK)
    start = jnp.concatenate([by_block, by_block], axis=2)
    four = jnp.arange(4, dtype=jnp.int32) ^ near
    position = lax.dynamic_slice_in_dim(index - begin, zh * 4 * rows, 4 * rows).astype(F32)
    inverse = ROPE_BASE ** (-(jnp.arange(head // 2, dtype=F32) * 2.0) / head)
    angle = (position[:, None] * inverse[None, :]).reshape(4, rows, head // 2)[four]
    cos_half, sin_half = jnp.cos(angle), jnp.sin(angle)
    cosine = jnp.concatenate([cos_half] * 4, axis=2)
    sine = jnp.concatenate([-sin_half, sin_half] * 2, axis=2)
    eight = jnp.arange(8, dtype=jnp.int32)
    places = jnp.concatenate([zh * 4 + four, (1 - zh) * 4 + four]).astype(jnp.int32)

    other = qkv_call(xa_near, qkv_w, 1, cosine, sine, gain_q, gain_k, head)
    (cotangent, ffn_own, gate_far, up_far), other = after(
        (cotangent, ffn_own, gate_far, up_far), other
    )
    dy = own_order(cotangent, y, c)
    got = swap(other, "zh", 1)
    dy_near = [dy, swap(dy, NEAR, 1), swap(dy, NEAR, 2)]
    own_y = swap(ffn_own, "y", 1)
    own = qkv_call(xa_near, qkv_w, 0, cosine, sine, gain_q, gain_k, head)
    (dy_near, ffn_own, gate_far, up_far, heads), own, got, own_y = after(
        (dy_near, ffn_own, gate_far, up_far, qkv_w[0]), own, got, own_y
    )

    context, log_total, qkv = attend_call(first, places, (own, got), start, head)
    down_far = swap(ffn_own[2], "zh", 1)
    out_w = jnp.concatenate([heads[:2, n:], heads[2:, n:]], axis=-1)
    out_w = [out_w] + [swap(out_w, NEAR, bit) for bit in (1, 2, 3)]
    gate_y = swap(gate_far, "y", 1)
    (dy_near, ffn_own, own_y, gate_far, up_far), context, down_far, gate_y, out_w = after(
        (dy_near, ffn_own, own_y, gate_far, up_far), context, down_far, gate_y, out_w
    )

    def to_heads(v):
        return lax.all_to_all(v, TENSOR, 0, 0, tiled=True)

    context_rows = to_heads(context.reshape(-1, rows, nq))
    dy_near.append(swap(dy_near[2], NEAR, 1))
    up_y, down_y = swap(up_far, "y", 1), swap(down_far, "y", 1)
    out_w = jnp.stack(out_w)
    out_w = [v.reshape((8,) + v.shape[2:]) for v in (out_w, swap(out_w, "c", 1))]
    w = [ffn_own, own_y, gate_far, gate_y, up_far, up_y, down_far, down_y]
    own_c, own_yc = swap(ffn_own, "c", 1), swap(own_y, "c", 1)
    w, context_rows, dy_near, own_c, own_yc, out_w = after(
        w, context_rows, dy_near, own_c, own_yc, out_w
    )

    hidden, xf = project_call(places, context_rows, out_w, x, gain_f)
    ffn_w = [w[0], own_c, w[1], own_yc]
    for k in (0, 1, 2):
        far, far_y = w[2 + 2 * k : 4 + 2 * k]
        ffn_w += [far, swap(far, "c", 1), far_y, swap(far_y, "c", 1)]

    xf_near = [xf] + [swap(xf, NEAR, bit) for bit in (1, 2, 3)]
    acts_0, out_0, d_xf_0 = ffn_call(xf_near[:1], dy_near[:1], ffn_w)
    acts_1, out_1, d_xf_1, acts_2, out_2, d_xf_2 = ffn_call(xf_near[1:3], dy_near[1:3], ffn_w)
    acts_3, out_3, d_xf_3 = ffn_call(xf_near[3:], dy_near[3:], ffn_w)
    d_xf = [d_xf_0, swap(d_xf_1, NEAR, 1), swap(d_xf_2, NEAR, 2), swap(d_xf_3, NEAR, 3)]
    acts = [acts_0, acts_1, acts_2, acts_3]
    keep_1, send_1 = ffn_grad_call(acts, xf_near, dy_near, 1)
    keep_0, send_0 = ffn_grad_call(acts, xf_near, dy_near, 0)
    (out_0, out_1, out_2, out_3), d_xf, keep_1, send_1, keep_0, send_0 = after(
        (out_0, out_1, out_2, out_3), d_xf, keep_1, send_1, keep_0, send_0
    )

    d_context_rows, out_keep, out_send, d_hidden, ffn_gain_part = project_back_call(
        places, context_rows, out_w, hidden, gain_f, dy, d_xf
    )
    d_context = to_heads(d_context_rows).reshape(total_rows, nq)
    ffn_1 = add_swapped(keep_1, send_1, "c", 1).astype(BF16)
    gate_1 = add_swapped(*halves(ffn_1[0]), "y", 1).astype(BF16)
    out_grad = add_swapped(out_keep, out_send, "c", 1).astype(BF16)
    (out_1, out_2, out_3, keep_0, ffn_1), d_context, gate_1, out_grad = after(
        (out_1, out_2, out_3, keep_0, ffn_1), d_context, gate_1, out_grad
    )

    place = jnp.where(eight // 4 == zh, 4, 0) + ((eight % 4) ^ near)
    d_qkv = attend_back_call(
        first, place.astype(jnp.int32), qkv, context, d_context, start, log_total, head
    )
    ffn_0 = add_swapped(keep_0, send_0, "c", 1).astype(BF16)
    up_1 = add_swapped(*halves(ffn_1[1]), "y", 1).astype(BF16)
    gate_part = swap(gate_1, "zh", 1)
    ffn_out = [out_0, swap(out_1, NEAR, 1), swap(out_2, NEAR, 2)]
    (ffn_1, out_3, out_grad), d_qkv, ffn_0, up_1, gate_part, *ffn_out = after(
        (ffn_1, out_3, out_grad), d_qkv, ffn_0, up_1, gate_part, *ffn_out
    )

    got = swap(d_qkv[:4], "zh", 1)
    ffn_0 = add_swapped(*halves(ffn_0), "y", 1)
    out_grad = out_grad.reshape((4, 2) + out_grad.shape[1:])
    out_grad = out_grad[0].astype(F32) + sum(
        swap(out_grad[bit], NEAR, bit).astype(F32) for bit in (1, 2, 3)
    )
    (ffn_1, up_1, out_3, d_qkv), got, ffn_0, out_grad = after(
        (ffn_1, up_1, out_3, d_qkv), got, ffn_0, out_grad.astype(BF16)
    )

    gains = (gain_q, gain_k, gain_a)
    xa = [xa_near[b] for b in (3, 1)]
    *d_xa, qkv_keep, qkv_send, head_parts, attn_gain_part = qkv_back_call(
        (d_qkv[4:], got), xa_near, qkv_w, cosine, sine, gains, head
    )
    down_1 = add_swapped(*halves(ffn_1[2]), "y", 1).astype(BF16)
    out_grad = add_swapped(*halves(out_grad), "y", 1)
    up_down = jnp.stack([up_1, down_1])
    (up_down, out_3), d_xa, qkv_send, out_grad, attn_gain_part = after(
        (up_down, out_3), d_xa, qkv_send, out_grad, attn_gain_part
    )

    d_xa = [d_xa[0]] + [swap(d_xa[bit], NEAR, bit) for bit in (1, 2, 3)]
    qkv_grad = add_swapped(qkv_keep, qkv_send, "c", 1).astype(BF16)
    up_down = swap(up_down, "zh", 1)
    (qkv_grad, out_grad, out_3, attn_gain_part), d_xa, up_down = after(
        (qkv_grad, out_grad, out_3, attn_gain_part), d_xa, up_down
    )

    ffn_out.append(swap(out_3, NEAR, 3))
    d = x.shape[1]
    gains = total_of(
        jnp.concatenate(
            [
                arrays_order(attn_gain_part, y, c)[0],
                arrays_order(ffn_gain_part, y, c)[0],
                head_parts[0, :head] + head_parts[0, head:],
                head_parts[1, :head],
            ]
        ).reshape(-1, 128)
    ).reshape(-1)
    own, far = halves(qkv_grad)
    qkv_grad = own[0].astype(F32) + swap(far[0], "y", 1).astype(F32)
    qkv_grad = qkv_grad + swap(own[1], "zh", 1).astype(F32)
    qkv_grad = qkv_grad + swap(far[1], ("y", "zh"), 3).astype(F32)
    out_grad = add_swapped(out_grad[0], out_grad[1].astype(BF16), "zh", 1)
    d_xa = sum(v.astype(F32) for v in d_xa)
    x_back, _ = norm_back(x, x_factor, gain_a, d_xa)
    input_grad = arrays_order((d_hidden + x_back).astype(BF16), y, c)
    block_out = arrays_order((hidden + sum(v.astype(F32) for v in ffn_out)).astype(BF16), y, c)
    qkv_grad = scatter_runs(qkv_grad)
    out_grad = scatter_runs(out_grad)
    ffn_grad = [
        scatter_runs(ffn_0[k] + part.astype(F32))
        for k, part in enumerate((gate_part, up_down[0], up_down[1]))
    ]

    return (
        block_out,
        input_grad,
        gains[:d],
        qkv_grad[:nq].T,
        qkv_grad[nq : nq + nk].T,
        qkv_grad[nq + nk :].T,
        out_grad,
        gains[2 * d : 2 * d + head],
        gains[2 * d + head :],
        gains[d : 2 * d],
        ffn_grad[0].T,
        ffn_grad[1].T,
        ffn_grad[2],
    )


def solution(mesh):
    dp, tensor = mesh.shape["dp"], mesh.shape["tensor"]
    cut = Mesh(
        mesh.devices.reshape(dp // 4, 2, 2, tensor // 4, 2, 2), ("r", "y", "c", "zh", "zl", "x")
    )
    data, model = ("r", "y", "c"), TENSOR
    both = data + model
    rows, wide, tall = P(both, None), P(data, model), P(model, data)
    in_specs = (
        rows, P(data, None), rows, P(), wide, wide, wide, tall, P(), P(), P(), wide, wide, tall
    )
    out_specs = (
        rows, rows, P(), wide, wide, wide, tall, P(), P(), P(), wide, wide, tall
    )
    return jax.shard_map(
        per_device, mesh=cut, in_specs=in_specs, out_specs=out_specs, check_vma=False
    )
```

profile of v0, /device:TPU:0, one launch (start us, length us, event | category | flops | bytes accessed | tf_op | source)
XLA Modules:
  0.0 387.9 jit_solution(17275808599123306135)
XLA Ops:
  2.5 5.1 %collective-permute-start.5 = (bf16[384,256]{1,0:T(8,128)(2,1)S(1)}, bf16[384,256]{1,0:T(8,128)(2,1)S(1)}, u32[]{:S(2)}, u32[]{:S(2)}) collective-permute-start(bf16[384,256]{1,0:T(8,128)(2,1)S(1)} %pad_maximum_fusion.11), channel_id=1, source_target_pairs={{0,20},{4,16},{16,4},{20,0},{1,21},{5,17},{17,5},{21,1},{2,22},{6,... | collective-permute-start | bytes 589832 | tf_op jit(solution)/shard_map/ppermute | solution.py:41
  20.4 17.7 %collective-permute-done.3 = bf16[384,256]{1,0:T(8,128)(2,1)} collective-permute-done((bf16[384,256]{1,0:T(8,128)(2,1)S(1)}, bf16[384,256]{1,0:T(8,128)(2,1)}, u32[]{:S(2)}, u32[]{:S(2)}) %collective-permute-start.3) | collective-permute-done | bytes 196640 | tf_op jit(solution)/shard_map/ppermute | solution.py:41
  41.8 1.9 fusion.15
  44.7 13.7 %collective-permute-done.8.refs_10_.refs_12_ = bf16[576,256]{1,0:T(8,128)(2,1)S(1)} collective-permute-done((bf16[576,256]{1,0:T(8,128)(2,1)S(1)}, bf16[576,256]{1,0:T(8,128)(2,1)S(1)}, u32[]{:S(2)}, u32[]{:S(2)}) %collective-permute-start.8) | collective-permute-done | bytes 294944 | tf_op jit(solution)/shard_map/ppermute | solution.py:41
  59.1 2.9 qkv.2
  72.9 2.1 qkv.3.refs_0_
  75.0 10.5 %collective-permute-done.10.refs_3_.refs_10_ = bf16[256,1024]{1,0:T(8,128)(2,1)} collective-permute-done((bf16[256,1024]{1,0:T(8,128)(2,1)S(1)}, bf16[256,1024]{1,0:T(8,128)(2,1)}, u32[]{:S(2)}, u32[]{:S(2)}) %collective-permute-start.10) | collective-permute-done | bytes 524320 | tf_op jit(solution)/shard_map/ppermute | solution.py:41
  85.5 4.6 %collective-permute-done.11.refs_1_ = bf16[4,256,256]{2,1,0:T(8,128)(2,1)} collective-permute-done((bf16[4,256,256]{2,1,0:T(8,128)(2,1)}, bf16[4,256,256]{2,1,0:T(8,128)(2,1)}, u32[]{:S(2)}, u32[]{:S(2)}) %collective-permute-start.11) | collective-permute-done | bytes 524320 | tf_op jit(solution)/shard_map/ppermute | solution.py:41
  90.3 2.2 collective-permute-start.16
  96.9 11.4 %attend.1 = (bf16[2048,128]{1,0:T(8,128)(2,1)S(1)}, f32[8,1,512]{2,1,0:T(1,128)S(1)}, bf16[2048,256]{1,0:T(8,128)(2,1)S(1)}) custom-call(s32[8]{0:T(128)S(1)} %and_select_fusion.2.first, s32[8]{0:T(128)S(1)} %pad_add_fusion.1.at, bf16[4,256,256]{2,1,0:T(8,128)(2,1)S(1)} %copy-done.45, bf16[4,256,256]{2,1,0:T(8,128)(2,1)} %collective-permute-done.11.refs_1_, ...), custom_call_target="tpu_custom_call" | custom-call | tf_op jit(solution)/shard_map/attend/pallas_call | solution.py:217
  113.0 5.4 %all-to-all-start = ((bf16[8,256,128]{2,1,0:T(8,128)(2,1)}), bf16[8,256,128]{2,1,0:T(8,128)(2,1)}, u32[]{:S(2)}, u32[]{:S(2)}) async-start(bf16[8,256,128]{2,1,0:T(8,128)(2,1)} %bitcast.97), calls=%async_computation | async-start | bytes 1048576 | tf_op jit(solution)/shard_map/all_to_all | solution.py:652
  119.1 2.0 collective-permute-start.20
  121.1 7.4 %collective-permute-done.18.refs_12_.refs_14_ = bf16[576,256]{1,0:T(8,128)(2,1)} collective-permute-done((bf16[576,256]{1,0:T(8,128)(2,1)}, bf16[576,256]{1,0:T(8,128)(2,1)}, u32[]{:S(2)}, u32[]{:S(2)}) %collective-permute-start.18) | collective-permute-done | bytes 294944 | tf_op jit(solution)/shard_map/ppermute | solution.py:41
  128.7 2.2 fusion.12.x
  130.9 6.0 %collective-permute-done.19.refs_16_.refs_18_ = bf16[576,256]{1,0:T(8,128)(2,1)S(1)} collective-permute-done((bf16[576,256]{1,0:T(8,128)(2,1)}, bf16[576,256]{1,0:T(8,128)(2,1)S(1)}, u32[]{:S(2)}, u32[]{:S(2)}) %collective-permute-start.19) | collective-permute-done | bytes 294944 | tf_op jit(solution)/shard_map/ppermute | solution.py:41
  144.2 2.4 project.1
  146.6 1.9 collective-permute-start.32
  152.2 10.2 %collective-permute-done.32.refs_0_.refs_7_ = bf16[256,1024]{1,0:T(8,128)(2,1)S(1)} collective-permute-done((bf16[256,1024]{1,0:T(8,128)(2,1)S(1)}, bf16[256,1024]{1,0:T(8,128)(2,1)S(1)}, u32[]{:S(2)}, u32[]{:S(2)}) %collective-permute-start.32) | collective-permute-done | bytes 524320 | tf_op jit(solution)/shard_map/ppermute | solution.py:41
  162.5 6.7 %ffn.5 = (bf16[3,2,256,576]{3,2,1,0:T(8,128)(2,1)S(1)}, bf16[256,1024]{1,0:T(8,128)(2,1)S(1)}, bf16[256,1024]{1,0:T(8,128)(2,1)S(1)}) custom-call(bf16[256,1024]{1,0:T(8,128)(2,1)S(1)} %collective-permute-done.32.refs_0_.refs_7_, bf16[256,1024]{1,0:T(8,128)(2,1)S(1)} %copy-done.14, bf16[3,576,256]{2,1,0:T(8,128)(2,1)S(1)} %pad_maximum_fusion.1.refs_2_.refs_4_, ...), custom_call_target="tpu_custom_call" | custom-call | tf_op jit(solution)/shard_map/ffn/pallas_call | solution.py:512
  173.1 13.4 %ffn.4 = (bf16[3,2,256,576]{3,2,1,0:T(8,128)(2,1)S(1)}, bf16[256,1024]{1,0:T(8,128)(2,1)S(1)}, bf16[256,1024]{1,0:T(8,128)(2,1)S(1)}, bf16[3,2,256,576]{3,2,1,0:...) custom-call(bf16[256,1024]{1,0:T(8,128)(2,1)S(1)} %collective-permute-done.30.refs_0_.refs_5_, ...), custom_call_target="tpu_custom_call" | custom-call | tf_op jit(solution)/shard_map/ffn/pallas_call | solution.py:512
  190.1 6.7 %ffn.3 = (bf16[3,2,256,576]{3,2,1,0:T(8,128)(2,1)S(1)}, bf16[256,1024]{1,0:T(8,128)(2,1)S(1)}, bf16[256,1024]{1,0:T(8,128)(2,1)S(1)}) custom-call(bf16[256,1024]{1,0:T(8,128)(2,1)S(1)} %get-tuple-element.218.refs_0_.refs_4_, bf16[256,1024]{1,0:T(8,128)(2,1)S(1)} %pad_maximum_fusion.7.refs_1_.refs_8_.dy, ...), custom_call_target="tpu_custom_call" | custom-call | tf_op jit(solution)/shard_map/ffn/pallas_call | solution.py:512
  197.6 7.4 %ffn_grad.3 = (bf16[3,576,512]{2,1,0:T(8,128)(2,1)S(1)}, bf16[3,576,512]{2,1,0:T(8,128)(2,1)}) custom-call(bf16[3,2,256,576]{3,2,1,0:T(8,128)(2,1)S(1)} %get-tuple-element.241.refs_0_, bf16[3,2,256,576]{3,2,1,0:T(8,128)(2,1)S(1)} %get-tuple-element.242.refs_1_, bf16[3,2,256,576]{3,2,1,0:T(8,128)(2,1)S(1)} %copy-done.12, bf16[3,2,256,576]{3,2,1,0:T(8,128)(2,1)} %copy-done.11, ...), custom_call_target="tpu_custom_call" | custom-call | tf_op jit(solution)/shard_map/ffn_grad/pallas_call | solution.py:543
  206.3 7.7 %ffn_grad.2 = (bf16[3,576,512]{2,1,0:T(8,128)(2,1)S(1)}, bf16[3,576,512]{2,1,0:T(8,128)(2,1)}) custom-call(bf16[3,2,256,576]{3,2,1,0:T(8,128)(2,1)S(1)} %get-tuple-element.241.refs_0_, bf16[3,2,256,576]{3,2,1,0:T(8,128)(2,1)S(1)} %get-tuple-element.242.refs_1_, bf16[3,2,256,576]{3,2,1,0:T(8,128)(2,1)S(1)} %copy-done.12, bf16[3,2,256,576]{3,2,1,0:T(8,128)(2,1)} %copy-done.11, ...), custom_call_target="tpu_custom_call" | custom-call | tf_op jit(solution)/shard_map/ffn_grad/pallas_call | solution.py:543
  215.3 4.2 %project_back.1 = (bf16[8,256,128]{2,1,0:T(8,128)(2,1)}, bf16[8,128,512]{2,1,0:T(8,128)(2,1)S(1)}, bf16[8,128,512]{2,1,0:T(8,128)(2,1)}, f32[256,1024]{1,0:T(8,128)S(1)}, f32[1,1024]{1,0:T(1,128)S(1)}) custom-call(s32[8]{0:T(128)S(1)} %copy-done.69, bf16[8,256,128]{2,1,0:T(8,128)(2,1)} %all-to-all-done.context, bf16[8,128,512]{2,1,0:T(8,128)(2,1)S(1)} %bitcast.96, ...), custom_call_target="tpu_custom_call" | custom-call | tf_op jit(solution)/shard_map/project_back/pallas_call | solution.py:404
  222.6 4.5 %all-to-all-start.1 = ((bf16[8,256,128]{2,1,0:T(8,128)(2,1)}), bf16[8,256,128]{2,1,0:T(8,128)(2,1)S(1)}, u32[]{:S(2)}, u32[]{:S(2)}) async-start(bf16[8,256,128]{2,1,0:T(8,128)(2,1)} %get-tuple-element.259), calls=%async_computation.1 | async-start | bytes 1048576 | tf_op jit(solution)/shard_map/all_to_all | solution.py:652
  227.2 2.5 add_convert_fusion.1
  231.6 2.6 add_convert_fusion.2
  234.2 4.8 %collective-permute-done.37 = bf16[576,256]{1,0:T(8,128)(2,1)S(1)} collective-permute-done((bf16[576,256]{1,0:T(8,128)(2,1)S(1)}, bf16[576,256]{1,0:T(8,128)(2,1)S(1)}, u32[]{:S(2)}, u32[]{:S(2)}) %collective-permute-start.37) | collective-permute-done | bytes 294944 | tf_op jit(solution)/shard_map/ppermute | solution.py:41
  239.1 3.3 all-to-all-done.1
  243.8 2.0 collective-permute-start.43
  247.7 2.0 add_convert_fusion
  249.7 14.6 %attend_back.1 = bf16[8,256,256]{2,1,0:T(8,128)(2,1)S(1)} custom-call(s32[8]{0:T(128)S(1)} %copy-done.73, s32[8]{0:T(128)S(1)} %fusion.8.to, bf16[2048,256]{1,0:T(8,128)(2,1)S(1)} %copy-done.54, bf16[2048,128]{1,0:T(8,128)(2,1)S(1)} %copy-done.43, bf16[2048,128]{1,0:T(8,128)(2,1)S(1)} %bitcast.98, s32[8,1,512]{2,1,0:T(1,128)S(1)} %pad_add_fusion.refs_2_.start, ...), custom_call_target="tpu_custom_call" | custom-call | tf_op jit(solution)/shard_map/attend_back/pallas_call | solution.py:306
  267.4 2.0 collective-permute-start.47
  270.4 7.1 %collective-permute-done.46 = bf16[2,128,512]{2,1,0:T(8,128)(2,1)S(1)} collective-permute-done((bf16[2,128,512]{2,1,0:T(8,128)(2,1)S(1)}, bf16[2,128,512]{2,1,0:T(8,128)(2,1)S(1)}, u32[]{:S(2)}, u32[]{:S(2)}) %collective-permute-start.46) | collective-permute-done | bytes 262176 | tf_op jit(solution)/shard_map/ppermute | solution.py:41
  277.5 7.9 %collective-permute-done.48 = bf16[2,128,512]{2,1,0:T(8,128)(2,1)S(1)} collective-permute-done((bf16[2,128,512]{2,1,0:T(8,128)(2,1)S(1)}, bf16[2,128,512]{2,1,0:T(8,128)(2,1)S(1)}, u32[]{:S(2)}, u32[]{:S(2)}) %collective-permute-start.48) | collective-permute-done | bytes 262176 | tf_op jit(solution)/shard_map/ppermute | solution.py:41
  285.4 5.5 %collective-permute-done.47 = bf16[2,128,512]{2,1,0:T(8,128)(2,1)S(1)} collective-permute-done((bf16[2,128,512]{2,1,0:T(8,128)(2,1)S(1)}, bf16[2,128,512]{2,1,0:T(8,128)(2,1)S(1)}, u32[]{:S(2)}, u32[]{:S(2)}) %collective-permute-start.47) | collective-permute-done | bytes 262176 | tf_op jit(solution)/shard_map/ppermute | solution.py:41
  291.4 4.4 %collective-permute-done.44.refs_1_ = bf16[4,256,256]{2,1,0:T(8,128)(2,1)S(1)} collective-permute-done((bf16[4,256,256]{2,1,0:T(8,128)(2,1)S(1)}, bf16[4,256,256]{2,1,0:T(8,128)(2,1)S(1)}, u32[]{:S(2)}, u32[]{:S(2)}) %collective-permute-start.44) | collective-permute-done | bytes 524320 | tf_op jit(solution)/shard_map/ppermute | solution.py:41
  299.2 5.7 %qkv_back.1 = (bf16[256,1024]{1,0:T(8,128)(2,1)S(1)}, bf16[256,1024]{1,0:T(8,128)(2,1)S(1)}, bf16[256,1024]{1,0:T(8,128)(2,1)S(1)}, bf16[256,1024]{1,0:T(8,128)(...) custom-call(bf16[4,256,256]{2,1,0:T(8,128)(2,1)S(1)} %slice.155.refs, ...), custom_call_target="tpu_custom_call" | custom-call | tf_op jit(solution)/shard_map/qkv_back/pallas_call | solution.py:466
  305.0 2.1 collective-permute-done.49
  312.1 9.7 %collective-permute-done.52 = bf16[256,1024]{1,0:T(8,128)(2,1)S(1)} collective-permute-done((bf16[256,1024]{1,0:T(8,128)(2,1)S(1)}, bf16[256,1024]{1,0:T(8,128)(2,1)S(1)}, u32[]{:S(2)}, u32[]{:S(2)}) %collective-permute-start.52) | collective-permute-done | bytes 524320 | tf_op jit(solution)/shard_map/ppermute | solution.py:41
  321.8 10.6 %collective-permute-done.53 = bf16[256,1024]{1,0:T(8,128)(2,1)S(1)} collective-permute-done((bf16[256,1024]{1,0:T(8,128)(2,1)S(1)}, bf16[256,1024]{1,0:T(8,128)(2,1)S(1)}, u32[]{:S(2)}, u32[]{:S(2)}) %collective-permute-start.53) | collective-permute-done | bytes 524320 | tf_op jit(solution)/shard_map/ppermute | solution.py:41
  332.4 14.4 %collective-permute-done.54 = bf16[256,1024]{1,0:T(8,128)(2,1)S(1)} collective-permute-done((bf16[256,1024]{1,0:T(8,128)(2,1)S(1)}, bf16[256,1024]{1,0:T(8,128)(2,1)S(1)}, u32[]{:S(2)}, u32[]{:S(2)}) %collective-permute-start.54) | collective-permute-done | bytes 524320 | tf_op jit(solution)/shard_map/ppermute | solution.py:41
  352.0 4.1 %all-to-all-start.2 = ((f32[32,17,128]{2,1,0:T(8,128)}), f32[32,17,128]{2,1,0:T(8,128)S(1)}, u32[]{:S(2)}, u32[]{:S(2)}) async-start(f32[32,17,128]{2,1,0:T(8,128)} %broadcast_in_dim.38), calls=%async_computation.2 | async-start | bytes 786432 | tf_op jit(solution)/shard_map/all_to_all | solution.py:88
  356.1 1.8 collective-permute-start.57
  358.0 2.4 collective-permute-start.59
  360.6 2.7 collective-permute-start.56
  366.6 11.5 %collective-permute-done.59 = bf16[256,256]{1,0:T(8,128)(2,1)S(1)} collective-permute-done((bf16[256,256]{1,0:T(8,128)(2,1)S(1)}, bf16[256,256]{1,0:T(8,128)(2,1)S(1)}, u32[]{:S(2)}, u32[]{:S(2)}) %collective-permute-start.59) | collective-permute-done | bytes 131104 | tf_op jit(solution)/shard_map/ppermute | solution.py:41
  381.0 2.5 collective-permute-done.56
  (397 shorter events, 99.0 us)
Async XLA Ops:
  2.5 14.3 %collective-permute-start.5 = (bf16[384,256]{1,0:T(8,128)(2,1)S(1)}, bf16[384,256]{1,0:T(8,128)(2,1)S(1)}, u32[]{:S(2)}, u32[]{:S(2)}) collective-permute-start(bf16[384,256]{1,0:T(8,128)(2,1)S(1)} %pad_maximum_fusion.11), channel_id=1, source_target_pairs={{0,20},{4,16},{16,4},{20,0},{1,21},{5,17},{17,5},{21,1},{2,22},{6,... | collective-permute-start | bytes 589832 | tf_op jit(solution)/shard_map/ppermute | solution.py:41
  7.5 12.8 %collective-permute-start.4 = (bf16[384,256]{1,0:T(8,128)(2,1)S(1)}, bf16[384,256]{1,0:T(8,128)(2,1)}, u32[]{:S(2)}, u32[]{:S(2)}) collective-permute-start(bf16[384,256]{1,0:T(8,128)(2,1)S(1)} %pad_maximum_fusion.11), channel_id=1, source_target_pairs={{0,16},{16,0},{1,17},{17,1},{2,18},{18,2},{3,19},{19,3},{4,20},{20... | collective-permute-start | bytes 589832 | tf_op jit(solution)/shard_map/ppermute | solution.py:41
  11.3 26.8 %collective-permute-start.1 = (bf16[256,1024]{1,0:T(8,128)(2,1)S(1)}, bf16[256,1024]{1,0:T(8,128)(2,1)S(1)}, u32[]{:S(2)}, u32[]{:S(2)}) collective-permute-start(bf16[256,1024]{1,0:T(8,128)(2,1)S(1)} %multiply_convert_fusion.refs_0_.refs_2_), channel_id=1, source_target_pairs={{0,2},{1,3},{2,0},{3,1},{4,6},{5,7},{6,4},{7,5},{8,10},{9,11},{10,... | collective-permute-start | bytes 1572872 | tf_op jit(solution)/shard_map/ppermute | solution.py:41
  12.9 25.2 %collective-permute-start = (bf16[256,1024]{1,0:T(8,128)(2,1)S(1)}, bf16[256,1024]{1,0:T(8,128)(2,1)S(1)}, u32[]{:S(2)}, u32[]{:S(2)}) collective-permute-start(bf16[256,1024]{1,0:T(8,128)(2,1)S(1)} %multiply_convert_fusion.refs_0_.refs_2_), channel_id=1, source_target_pairs={{0,1},{1,0},{2,3},{3,2},{4,5},{5,4},{6,7},{7,6},{8,9},{9,8},{10,11... | collective-permute-start | bytes 1572872 | tf_op jit(solution)/shard_map/ppermute | solution.py:41
  14.4 23.7 %collective-permute-start.2 = (bf16[576,256]{1,0:T(8,128)(2,1)}, bf16[576,256]{1,0:T(8,128)(2,1)S(1)}, u32[]{:S(2)}, u32[]{:S(2)}) collective-permute-start(bf16[576,256]{1,0:T(8,128)(2,1)} %bitcast.2), channel_id=1, source_target_pairs={{0,4},{4,0},{1,5},{5,1},{2,6},{6,2},{3,7},{7,3},{8,12},{12,8},{9,1... | collective-permute-start | bytes 884744 | tf_op jit(solution)/shard_map/ppermute | solution.py:41
  16.8 21.3 %collective-permute-start.3 = (bf16[384,256]{1,0:T(8,128)(2,1)S(1)}, bf16[384,256]{1,0:T(8,128)(2,1)}, u32[]{:S(2)}, u32[]{:S(2)}) collective-permute-start(bf16[384,256]{1,0:T(8,128)(2,1)S(1)} %pad_maximum_fusion.11), channel_id=1, source_target_pairs={{0,4},{4,0},{1,5},{5,1},{2,6},{6,2},{3,7},{7,3},{8,12},{12,8},{9,1... | collective-permute-start | bytes 589832 | tf_op jit(solution)/shard_map/ppermute | solution.py:41
  38.9 19.4 %collective-permute-start.6 = (bf16[256,1024]{1,0:T(8,128)(2,1)S(1)}, bf16[256,1024]{1,0:T(8,128)(2,1)S(1)}, u32[]{:S(2)}, u32[]{:S(2)}) collective-permute-start(bf16[256,1024]{1,0:T(8,128)(2,1)S(1)} %collective-permute-done.1.refs_2_.refs_4_), channel_id=1, source_target_pairs={{0,1},{1,0},{2,3},{3,2},{4,5},{5,4},{6,7},{7,6},{8,9},{9,8},{10,11... | collective-permute-start | bytes 1572872 | tf_op jit(solution)/shard_map/ppermute | solution.py:41
  41.6 16.8 %collective-permute-start.7 = (bf16[4,256,256]{2,1,0:T(8,128)(2,1)S(1)}, bf16[4,256,256]{2,1,0:T(8,128)(2,1)S(1)}, u32[]{:S(2)}, u32[]{:S(2)}) collective-permute-start(bf16[4,256,256]{2,1,0:T(8,128)(2,1)S(1)} %slice.182), channel_id=1, source_target_pairs={{0,8},{8,0},{1,9},{9,1},{2,10},{10,2},{3,11},{11,3},{4,12},{12,4},... | collective-permute-start | bytes 1572872 | tf_op jit(solution)/shard_map/ppermute | solution.py:41
  41.7 16.7 %collective-permute-start.8 = (bf16[576,256]{1,0:T(8,128)(2,1)S(1)}, bf16[576,256]{1,0:T(8,128)(2,1)S(1)}, u32[]{:S(2)}, u32[]{:S(2)}) collective-permute-start(bf16[576,256]{1,0:T(8,128)(2,1)S(1)} %slice_bitcast_fusion.4), channel_id=1, source_target_pairs={{0,4},{4,0},{1,5},{5,1},{2,6},{6,2},{3,7},{7,3},{8,12},{12,8},{9,1... | collective-permute-start | bytes 884744 | tf_op jit(solution)/shard_map/ppermute | solution.py:41
  62.1 28.1 %collective-permute-start.12 = (bf16[3,576,256]{2,1,0:T(8,128)(2,1)S(1)}, bf16[3,576,256]{2,1,0:T(8,128)(2,1)}, u32[]{:S(2)}, u32[]{:S(2)}) collective-permute-start(bf16[3,576,256]{2,1,0:T(8,128)(2,1)S(1)} %pad_maximum_fusion.1.refs_2_.refs_4_), channel_id=1, source_target_pairs={{0,16},{16,0},{1,17},{17,1},{2,18},{18,2},{3,19},{19,3},{4,20},{20... | collective-permute-start | bytes 2654216 | tf_op jit(solution)/shard_map/ppermute | solution.py:41
  63.2 22.3 %collective-permute-start.10 = (bf16[256,1024]{1,0:T(8,128)(2,1)S(1)}, bf16[256,1024]{1,0:T(8,128)(2,1)}, u32[]{:S(2)}, u32[]{:S(2)}) collective-permute-start(bf16[256,1024]{1,0:T(8,128)(2,1)S(1)} %pad_maximum_fusion.7.refs_1_.refs_8_.dy), channel_id=1, source_target_pairs={{0,2},{1,3},{2,0},{3,1},{4,6},{5,7},{6,4},{7,5},{8,10},{9,11},{10,... | collective-permute-start | bytes 1572872 | tf_op jit(solution)/shard_map/ppermute | solution.py:41
  63.2 22.2 %collective-permute-start.9 = (bf16[256,1024]{1,0:T(8,128)(2,1)S(1)}, bf16[256,1024]{1,0:T(8,128)(2,1)}, u32[]{:S(2)}, u32[]{:S(2)}) collective-permute-start(bf16[256,1024]{1,0:T(8,128)(2,1)S(1)} %pad_maximum_fusion.7.refs_1_.refs_8_.dy), channel_id=1, source_target_pairs={{0,1},{1,0},{2,3},{3,2},{4,5},{5,4},{6,7},{7,6},{8,9},{9,8},{10,11... | collective-permute-start | bytes 1572872 | tf_op jit(solution)/shard_map/ppermute | solution.py:41
  64.3 25.8 %collective-permute-start.11 = (bf16[4,256,256]{2,1,0:T(8,128)(2,1)}, bf16[4,256,256]{2,1,0:T(8,128)(2,1)}, u32[]{:S(2)}, u32[]{:S(2)}) collective-permute-start(bf16[4,256,256]{2,1,0:T(8,128)(2,1)} %qkv.2), channel_id=1, source_target_pairs={{0,4},{4,0},{1,5},{5,1},{2,6},{6,2},{3,7},{7,3},{8,12},{12,8},{9,1... | collective-permute-start | bytes 1572872 | tf_op jit(solution)/shard_map/ppermute | solution.py:41
  90.2 20.6 %collective-permute-start.17 = (bf16[2,128,512]{2,1,0:T(8,128)(2,1)S(1)}, bf16[2,128,512]{2,1,0:T(8,128)(2,1)}, u32[]{:S(2)}, u32[]{:S(2)}) collective-permute-start(bf16[2,128,512]{2,1,0:T(8,128)(2,1)S(1)} %pad_maximum_fusion.10), channel_id=1, source_target_pairs={{0,3},{1,2},{2,1},{3,0},{4,7},{5,6},{6,5},{7,4},{8,11},{9,10},{10,... | collective-permute-start | bytes 786440 | tf_op jit(solution)/shard_map/ppermute | solution.py:41
  90.3 20.5 %collective-permute-start.16 = (bf16[2,128,512]{2,1,0:T(8,128)(2,1)S(1)}, bf16[2,128,512]{2,1,0:T(8,128)(2,1)}, u32[]{:S(2)}, u32[]{:S(2)}) collective-permute-start(bf16[2,128,512]{2,1,0:T(8,128)(2,1)S(1)} %pad_maximum_fusion.10), channel_id=1, source_target_pairs={{0,2},{1,3},{2,0},{3,1},{4,6},{5,7},{6,4},{7,5},{8,10},{9,11},{10,... | collective-permute-start | bytes 786440 | tf_op jit(solution)/shard_map/ppermute | solution.py:41
  92.4 18.4 %collective-permute-start.15 = (bf16[2,128,512]{2,1,0:T(8,128)(2,1)S(1)}, bf16[2,128,512]{2,1,0:T(8,128)(2,1)}, u32[]{:S(2)}, u32[]{:S(2)}) collective-permute-start(bf16[2,128,512]{2,1,0:T(8,128)(2,1)S(1)} %pad_maximum_fusion.10), channel_id=1, source_target_pairs={{0,1},{1,0},{2,3},{3,2},{4,5},{5,4},{6,7},{7,6},{8,9},{9,8},{10,11... | collective-permute-start | bytes 786440 | tf_op jit(solution)/shard_map/ppermute | solution.py:41
  94.5 16.3 %collective-permute-start.13 = (bf16[576,256]{1,0:T(8,128)(2,1)}, bf16[576,256]{1,0:T(8,128)(2,1)S(1)}, u32[]{:S(2)}, u32[]{:S(2)}) collective-permute-start(bf16[576,256]{1,0:T(8,128)(2,1)} %slice_bitcast_fusion.3), channel_id=1, source_target_pairs={{0,4},{4,0},{1,5},{5,1},{2,6},{6,2},{3,7},{7,3},{8,12},{12,8},{9,1... | collective-permute-start | bytes 884744 | tf_op jit(solution)/shard_map/ppermute | solution.py:41
  94.5 16.4 %collective-permute-start.14 = (bf16[576,256]{1,0:T(8,128)(2,1)S(1)}, bf16[576,256]{1,0:T(8,128)(2,1)S(1)}, u32[]{:S(2)}, u32[]{:S(2)}) collective-permute-start(bf16[576,256]{1,0:T(8,128)(2,1)S(1)} %collective-permute-done.2.refs_6_.refs_8_), channel_id=1, source_target_pairs={{0,16},{16,0},{1,17},{17,1},{2,18},{18,2},{3,19},{19,3},{4,20},{20... | collective-permute-start | bytes 884744 | tf_op jit(solution)/shard_map/ppermute | solution.py:41
  112.9 27.6 %collective-permute-start.23 = (bf16[4,2,128,512]{3,2,1,0:T(8,128)(2,1)S(1)}, bf16[4,2,128,512]{3,2,1,0:T(8,128)(2,1)}, u32[]{:S(2)}, u32[]{:S(2)}) collective-permute-start(bf16[4,2,128,512]{3,2,1,0:T(8,128)(2,1)S(1)} %pad_maximum_fusion), channel_id=1, source_target_pairs={{0,8},{8,0},{1,9},{9,1},{2,10},{10,2},{3,11},{11,3},{4,12},{12,4},... | collective-permute-start | bytes 3145736 | tf_op jit(solution)/shard_map/ppermute | solution.py:41
  113.0 27.5 %all-to-all-start = ((bf16[8,256,128]{2,1,0:T(8,128)(2,1)}), bf16[8,256,128]{2,1,0:T(8,128)(2,1)}, u32[]{:S(2)}, u32[]{:S(2)}) async-start(bf16[8,256,128]{2,1,0:T(8,128)(2,1)} %bitcast.97), calls=%async_computation | async-start | bytes 1048576 | tf_op jit(solution)/shard_map/all_to_all | solution.py:652
  118.4 20.3 %collective-permute-start.21 = (bf16[3,576,256]{2,1,0:T(8,128)(2,1)S(1)}, bf16[3,576,256]{2,1,0:T(8,128)(2,1)S(1)}, u32[]{:S(2)}, u32[]{:S(2)}) collective-permute-start(bf16[3,576,256]{2,1,0:T(8,128)(2,1)S(1)} %pad_maximum_fusion.1.refs_2_.refs_4_), channel_id=1, source_target_pairs={{0,8},{8,0},{1,9},{9,1},{2,10},{10,2},{3,11},{11,3},{4,12},{12,4},... | collective-permute-start | bytes 2654216 | tf_op jit(solution)/shard_map/ppermute | solution.py:41
  118.7 20.9 %collective-permute-start.22 = (bf16[3,576,256]{2,1,0:T(8,128)(2,1)}, bf16[3,576,256]{2,1,0:T(8,128)(2,1)S(1)}, u32[]{:S(2)}, u32[]{:S(2)}) collective-permute-start(bf16[3,576,256]{2,1,0:T(8,128)(2,1)} %collective-permute-done.12.refs_4_.refs_6_), channel_id=1, source_target_pairs={{0,8},{8,0},{1,9},{9,1},{2,10},{10,2},{3,11},{11,3},{4,12},{12,4},... | collective-permute-start | bytes 2654216 | tf_op jit(solution)/shard_map/ppermute | solution.py:41
  119.1 18.9 %collective-permute-start.20 = (bf16[256,1024]{1,0:T(8,128)(2,1)}, bf16[256,1024]{1,0:T(8,128)(2,1)S(1)}, u32[]{:S(2)}, u32[]{:S(2)}) collective-permute-start(bf16[256,1024]{1,0:T(8,128)(2,1)} %collective-permute-done.10.refs_3_.refs_10_), channel_id=1, source_target_pairs={{0,1},{1,0},{2,3},{3,2},{4,5},{5,4},{6,7},{7,6},{8,9},{9,8},{10,11... | collective-permute-start | bytes 1572872 | tf_op jit(solution)/shard_map/ppermute | solution.py:41
  146.6 15.8 %collective-permute-start.32 = (bf16[256,1024]{1,0:T(8,128)(2,1)S(1)}, bf16[256,1024]{1,0:T(8,128)(2,1)S(1)}, u32[]{:S(2)}, u32[]{:S(2)}) collective-permute-start(bf16[256,1024]{1,0:T(8,128)(2,1)S(1)} %get-tuple-element.218.refs_0_.refs_4_), channel_id=1, source_target_pairs={{0,3},{1,2},{2,1},{3,0},{4,7},{5,6},{6,5},{7,4},{8,11},{9,10},{10,... | collective-permute-start | bytes 1572872 | tf_op jit(solution)/shard_map/ppermute | solution.py:41
  148.5 24.6 %collective-permute-start.31 = (bf16[256,1024]{1,0:T(8,128)(2,1)S(1)}, bf16[256,1024]{1,0:T(8,128)(2,1)S(1)}, u32[]{:S(2)}, u32[]{:S(2)}) collective-permute-start(bf16[256,1024]{1,0:T(8,128)(2,1)S(1)} %get-tuple-element.218.refs_0_.refs_4_), channel_id=1, source_target_pairs={{0,2},{1,3},{2,0},{3,1},{4,6},{5,7},{6,4},{7,5},{8,10},{9,11},{10,... | collective-permute-start | bytes 1572872 | tf_op jit(solution)/shard_map/ppermute | solution.py:41
  149.1 24.0 %collective-permute-start.30 = (bf16[256,1024]{1,0:T(8,128)(2,1)S(1)}, bf16[256,1024]{1,0:T(8,128)(2,1)S(1)}, u32[]{:S(2)}, u32[]{:S(2)}) collective-permute-start(bf16[256,1024]{1,0:T(8,128)(2,1)S(1)} %get-tuple-element.218.refs_0_.refs_4_), channel_id=1, source_target_pairs={{0,1},{1,0},{2,3},{3,2},{4,5},{5,4},{6,7},{7,6},{8,9},{9,8},{10,11... | collective-permute-start | bytes 1572872 | tf_op jit(solution)/shard_map/ppermute | solution.py:41
  171.3 44.0 %collective-permute-start.35 = (bf16[256,1024]{1,0:T(8,128)(2,1)S(1)}, bf16[256,1024]{1,0:T(8,128)(2,1)S(1)}, u32[]{:S(2)}, u32[]{:S(2)}) collective-permute-start(bf16[256,1024]{1,0:T(8,128)(2,1)S(1)} %get-tuple-element.240), channel_id=1, source_target_pairs={{0,3},{1,2},{2,1},{3,0},{4,7},{5,6},{6,5},{7,4},{8,11},{9,10},{10,... | collective-permute-start | bytes 1572872 | tf_op jit(solution)/shard_map/ppermute | solution.py:41
  188.1 27.1 %collective-permute-start.33 = (bf16[256,1024]{1,0:T(8,128)(2,1)S(1)}, bf16[256,1024]{1,0:T(8,128)(2,1)S(1)}, u32[]{:S(2)}, u32[]{:S(2)}) collective-permute-start(bf16[256,1024]{1,0:T(8,128)(2,1)S(1)} %get-tuple-element.238), channel_id=1, source_target_pairs={{0,1},{1,0},{2,3},{3,2},{4,5},{5,4},{6,7},{7,6},{8,9},{9,8},{10,11... | collective-permute-start | bytes 1572872 | tf_op jit(solution)/shard_map/ppermute | solution.py:41
  189.2 26.0 %collective-permute-start.34 = (bf16[256,1024]{1,0:T(8,128)(2,1)S(1)}, bf16[256,1024]{1,0:T(8,128)(2,1)S(1)}, u32[]{:S(2)}, u32[]{:S(2)}) collective-permute-start(bf16[256,1024]{1,0:T(8,128)(2,1)S(1)} %get-tuple-element.239), channel_id=1, source_target_pairs={{0,2},{1,3},{2,0},{3,1},{4,6},{5,7},{6,4},{7,5},{8,10},{9,11},{10,... | collective-permute-start | bytes 1572872 | tf_op jit(solution)/shard_map/ppermute | solution.py:41
  222.6 25.1 %collective-permute-start.39 = (bf16[3,576,512]{2,1,0:T(8,128)(2,1)}, bf16[3,576,512]{2,1,0:T(8,128)(2,1)}, u32[]{:S(2)}, u32[]{:S(2)}) collective-permute-start(bf16[3,576,512]{2,1,0:T(8,128)(2,1)} %get-tuple-element.269), channel_id=1, source_target_pairs={{0,8},{8,0},{1,9},{9,1},{2,10},{10,2},{3,11},{11,3},{4,12},{12,4},... | collective-permute-start | bytes 5308424 | tf_op jit(solution)/shard_map/ppermute | solution.py:41
  222.6 19.7 %all-to-all-start.1 = ((bf16[8,256,128]{2,1,0:T(8,128)(2,1)}), bf16[8,256,128]{2,1,0:T(8,128)(2,1)S(1)}, u32[]{:S(2)}, u32[]{:S(2)}) async-start(bf16[8,256,128]{2,1,0:T(8,128)(2,1)} %get-tuple-element.259), calls=%async_computation.1 | async-start | bytes 1048576 | tf_op jit(solution)/shard_map/all_to_all | solution.py:652
  242.3 22.1 %collective-permute-start.41 = (bf16[576,256]{1,0:T(8,128)(2,1)S(1)}, bf16[576,256]{1,0:T(8,128)(2,1)S(1)}, u32[]{:S(2)}, u32[]{:S(2)}) collective-permute-start(bf16[576,256]{1,0:T(8,128)(2,1)S(1)} %add_convert_fusion.8), channel_id=1, source_target_pairs={{0,4},{4,0},{1,5},{5,1},{2,6},{6,2},{3,7},{7,3},{8,12},{12,8},{9,1... | collective-permute-start | bytes 884744 | tf_op jit(solution)/shard_map/ppermute | solution.py:41
  242.4 22.0 %collective-permute-start.42 = (bf16[256,1024]{1,0:T(8,128)(2,1)}, bf16[256,1024]{1,0:T(8,128)(2,1)S(1)}, u32[]{:S(2)}, u32[]{:S(2)}) collective-permute-start(bf16[256,1024]{1,0:T(8,128)(2,1)} %copy-done.77), channel_id=1, source_target_pairs={{0,1},{1,0},{2,3},{3,2},{4,5},{5,4},{6,7},{7,6},{8,9},{9,8},{10,11... | collective-permute-start | bytes 1572872 | tf_op jit(solution)/shard_map/ppermute | solution.py:41
  243.8 20.7 %collective-permute-start.43 = (bf16[256,1024]{1,0:T(8,128)(2,1)}, bf16[256,1024]{1,0:T(8,128)(2,1)S(1)}, u32[]{:S(2)}, u32[]{:S(2)}) collective-permute-start(bf16[256,1024]{1,0:T(8,128)(2,1)} %copy-done.76), channel_id=1, source_target_pairs={{0,2},{1,3},{2,0},{3,1},{4,6},{5,7},{6,4},{7,5},{8,10},{9,11},{10,... | collective-permute-start | bytes 1572872 | tf_op jit(solution)/shard_map/ppermute | solution.py:41
  247.0 17.4 %collective-permute-start.40 = (bf16[576,256]{1,0:T(8,128)(2,1)S(1)}, bf16[576,256]{1,0:T(8,128)(2,1)S(1)}, u32[]{:S(2)}, u32[]{:S(2)}) collective-permute-start(bf16[576,256]{1,0:T(8,128)(2,1)S(1)} %split.181), channel_id=1, source_target_pairs={{0,16},{16,0},{1,17},{17,1},{2,18},{18,2},{3,19},{19,3},{4,20},{20... | collective-permute-start | bytes 884744 | tf_op jit(solution)/shard_map/ppermute | solution.py:41
  265.3 25.7 %collective-permute-start.45 = (bf16[3,576,256]{2,1,0:T(8,128)(2,1)S(1)}, bf16[3,576,256]{2,1,0:T(8,128)(2,1)S(1)}, u32[]{:S(2)}, u32[]{:S(2)}) collective-permute-start(bf16[3,576,256]{2,1,0:T(8,128)(2,1)S(1)} %split.149), channel_id=1, source_target_pairs={{0,16},{16,0},{1,17},{17,1},{2,18},{18,2},{3,19},{19,3},{4,20},{20... | collective-permute-start | bytes 2654216 | tf_op jit(solution)/shard_map/ppermute | solution.py:41
  266.2 19.2 %collective-permute-start.48 = (bf16[2,128,512]{2,1,0:T(8,128)(2,1)S(1)}, bf16[2,128,512]{2,1,0:T(8,128)(2,1)S(1)}, u32[]{:S(2)}, u32[]{:S(2)}) collective-permute-start(bf16[2,128,512]{2,1,0:T(8,128)(2,1)S(1)} %get-tuple-element.374), channel_id=1, source_target_pairs={{0,3},{1,2},{2,1},{3,0},{4,7},{5,6},{6,5},{7,4},{8,11},{9,10},{10,... | collective-permute-start | bytes 786440 | tf_op jit(solution)/shard_map/ppermute | solution.py:41
  267.4 23.5 %collective-permute-start.47 = (bf16[2,128,512]{2,1,0:T(8,128)(2,1)S(1)}, bf16[2,128,512]{2,1,0:T(8,128)(2,1)S(1)}, u32[]{:S(2)}, u32[]{:S(2)}) collective-permute-start(bf16[2,128,512]{2,1,0:T(8,128)(2,1)S(1)} %get-tuple-element.375), channel_id=1, source_target_pairs={{0,2},{1,3},{2,0},{3,1},{4,6},{5,7},{6,4},{7,5},{8,10},{9,11},{10,... | collective-permute-start | bytes 786440 | tf_op jit(solution)/shard_map/ppermute | solution.py:41
  269.4 26.3 %collective-permute-start.44 = (bf16[4,256,256]{2,1,0:T(8,128)(2,1)S(1)}, bf16[4,256,256]{2,1,0:T(8,128)(2,1)S(1)}, u32[]{:S(2)}, u32[]{:S(2)}) collective-permute-start(bf16[4,256,256]{2,1,0:T(8,128)(2,1)S(1)} %slice.150), channel_id=1, source_target_pairs={{0,4},{4,0},{1,5},{5,1},{2,6},{6,2},{3,7},{7,3},{8,12},{12,8},{9,1... | collective-permute-start | bytes 1572872 | tf_op jit(solution)/shard_map/ppermute | solution.py:41
  307.4 39.4 %collective-permute-start.55 = (bf16[2,576,256]{2,1,0:T(8,128)(2,1)S(1)}, bf16[2,576,256]{2,1,0:T(8,128)(2,1)S(1)}, u32[]{:S(2)}, u32[]{:S(2)}) collective-permute-start(bf16[2,576,256]{2,1,0:T(8,128)(2,1)S(1)} %pad_maximum_fusion.3), channel_id=1, source_target_pairs={{0,4},{4,0},{1,5},{5,1},{2,6},{6,2},{3,7},{7,3},{8,12},{12,8},{9,1... | collective-permute-start | bytes 1769480 | tf_op jit(solution)/shard_map/ppermute | solution.py:41
  307.5 14.3 %collective-permute-start.52 = (bf16[256,1024]{1,0:T(8,128)(2,1)S(1)}, bf16[256,1024]{1,0:T(8,128)(2,1)S(1)}, u32[]{:S(2)}, u32[]{:S(2)}) collective-permute-start(bf16[256,1024]{1,0:T(8,128)(2,1)S(1)} %get-tuple-element.301), channel_id=1, source_target_pairs={{0,1},{1,0},{2,3},{3,2},{4,5},{5,4},{6,7},{7,6},{8,9},{9,8},{10,11... | collective-permute-start | bytes 1572872 | tf_op jit(solution)/shard_map/ppermute | solution.py:41
  307.9 24.6 %collective-permute-start.53 = (bf16[256,1024]{1,0:T(8,128)(2,1)S(1)}, bf16[256,1024]{1,0:T(8,128)(2,1)S(1)}, u32[]{:S(2)}, u32[]{:S(2)}) collective-permute-start(bf16[256,1024]{1,0:T(8,128)(2,1)S(1)} %get-tuple-element.302), channel_id=1, source_target_pairs={{0,2},{1,3},{2,0},{3,1},{4,6},{5,7},{6,4},{7,5},{8,10},{9,11},{10,... | collective-permute-start | bytes 1572872 | tf_op jit(solution)/shard_map/ppermute | solution.py:41
  309.6 37.2 %collective-permute-start.54 = (bf16[256,1024]{1,0:T(8,128)(2,1)S(1)}, bf16[256,1024]{1,0:T(8,128)(2,1)S(1)}, u32[]{:S(2)}, u32[]{:S(2)}) collective-permute-start(bf16[256,1024]{1,0:T(8,128)(2,1)S(1)} %get-tuple-element.303), channel_id=1, source_target_pairs={{0,3},{1,2},{2,1},{3,0},{4,7},{5,6},{6,5},{7,4},{8,11},{9,10},{10,... | collective-permute-start | bytes 1572872 | tf_op jit(solution)/shard_map/ppermute | solution.py:41
  351.1 14.0 %collective-permute-start.60 = (bf16[128,256]{1,0:T(8,128)(2,1)}, bf16[128,256]{1,0:T(8,128)(2,1)}, u32[]{:S(2)}, u32[]{:S(2)}) collective-permute-start(bf16[128,256]{1,0:T(8,128)(2,1)} %fusion.4), channel_id=1, source_target_pairs={{0,4},{4,0},{1,5},{5,1},{2,6},{6,2},{3,7},{7,3},{8,12},{12,8},{9,1... | collective-permute-start | bytes 196616 | tf_op jit(solution)/shard_map/ppermute | solution.py:41
  352.0 34.2 %all-to-all-start.2 = ((f32[32,17,128]{2,1,0:T(8,128)}), f32[32,17,128]{2,1,0:T(8,128)S(1)}, u32[]{:S(2)}, u32[]{:S(2)}) async-start(f32[32,17,128]{2,1,0:T(8,128)} %broadcast_in_dim.38), calls=%async_computation.2 | async-start | bytes 786432 | tf_op jit(solution)/shard_map/all_to_all | solution.py:88
  358.0 20.1 %collective-permute-start.59 = (bf16[256,256]{1,0:T(8,128)(2,1)S(1)}, bf16[256,256]{1,0:T(8,128)(2,1)S(1)}, u32[]{:S(2)}, u32[]{:S(2)}) collective-permute-start(bf16[256,256]{1,0:T(8,128)(2,1)S(1)} %get-tuple-element.379), channel_id=1, source_target_pairs={{0,20},{4,16},{16,4},{20,0},{1,21},{5,17},{17,5},{21,1},{2,22},{6,... | collective-permute-start | bytes 393224 | tf_op jit(solution)/shard_map/ppermute | solution.py:41
  360.3 19.2 %collective-permute-start.58 = (bf16[256,256]{1,0:T(8,128)(2,1)S(1)}, bf16[256,256]{1,0:T(8,128)(2,1)S(1)}, u32[]{:S(2)}, u32[]{:S(2)}) collective-permute-start(bf16[256,256]{1,0:T(8,128)(2,1)S(1)} %get-tuple-element.380), channel_id=1, source_target_pairs={{0,4},{4,0},{1,5},{5,1},{2,6},{6,2},{3,7},{7,3},{8,12},{12,8},{9,1... | collective-permute-start | bytes 393224 | tf_op jit(solution)/shard_map/ppermute | solution.py:41
  360.6 22.9 %collective-permute-start.56 = (bf16[256,1024]{1,0:T(8,128)(2,1)S(1)}, bf16[256,1024]{1,0:T(8,128)(2,1)}, u32[]{:S(2)}, u32[]{:S(2)}) collective-permute-start(bf16[256,1024]{1,0:T(8,128)(2,1)S(1)} %copy-done.75), channel_id=1, source_target_pairs={{0,3},{1,2},{2,1},{3,0},{4,7},{5,6},{6,5},{7,4},{8,11},{9,10},{10,... | collective-permute-start | bytes 1572872 | tf_op jit(solution)/shard_map/ppermute | solution.py:41
  (120 other events, 1027.8 us)
where the time goes:
time: 395 us; the launch traced here: 388 us
  waiting for transfers between devices  159 us (40%)
  Pallas kernels  85.3 us (22%)
  starting transfers between devices  69.5 us (18%)
  local copies, waits for them, and re-layouts  42.1 us (11%)
  other arithmetic  29.6 us (7%)
    ppermute x61, waiting for transfers between devices, swap(): return lax.ppermute(v, axes, [(i, i ^ bit) for i in range(size)])  156 us
    ppermute x61, starting transfers between devices, swap(): return lax.ppermute(v, axes, [(i, i ^ bit) for i in range(size)])  55.4 us
    unnamed x210, local copies, waits for them, and re-layouts  31.9 us
    pallas_call x3, Pallas kernels, ffn_call(): pl.pallas_call(functools.partial(ffn_kernel, count), out_shape=[jax.Shape...  26.8 us
    pallas_call x2, Pallas kernels, ffn_grad_call(): pl.pallas_call(ffn_grad_kernel, grid=(three,), in_specs=[by_kind] * 4 + [...  15.1 us
    pallas_call x1, Pallas kernels, attend_back_call(): pl.pallas_call(functools.partial(attend_back_kernel, head), grid_spec=plt...  14.6 us
    pallas_call x1, Pallas kernels, attend_call(): pl.pallas_call(functools.partial(attend_kernel, head), grid_spec=pltpu.Pr...  11.4 us
    all_to_all x2, starting transfers between devices, to_heads(): return lax.all_to_all(v, TENSOR, 0, 0, tiled=True)  9.96 us
  transfers between devices with their start and end apart: 64, of which 24 were waited for; matrix products, arithmetic and copies ran while one was open for 9% of the time, Pallas kernels for 21%

commit v1 on v0

--- a/solution.py
+++ b/solution.py
@@ -598,14 +598,14 @@
     )
     ffn_own = gather_runs(jnp.stack([gate_weight.T, up_weight.T, down_weight]))
     xa_near = [xa, swap(xa, NEAR, 1), swap(xa, NEAR, 2)]
-    heads = [shard, swap(shard, "zh", 1), swap(shard, "y", 1), swap(shard, ("y", "zh"), 3)]
+    shard_far = swap(shard, "zh", 1)
+    heads = jnp.stack([shard, shard_far, swap(shard, "y", 1), swap(shard_far, "y", 1)])
+    qkv_w = (heads, swap(heads[:, :n], "c", 1))
     gate_far = swap(ffn_own[0], "zh", 1)
-    (xa_near, ffn_own), gate_far, *heads = after((xa_near, ffn_own), gate_far, *heads)
+    (xa_near, ffn_own), gate_far, qkv_w = after((xa_near, ffn_own), gate_far, qkv_w)
     xa_near.append(swap(xa_near[2], NEAR, 1))
-    heads = jnp.stack(heads)
-    qkv_w = (heads, swap(heads[:, :n], "c", 1))
     up_far = swap(ffn_own[1], "zh", 1)
-    (ffn_own, xa_near, gate_far), qkv_w, up_far = after((ffn_own, xa_near, gate_far), qkv_w, up_far)
+    (ffn_own, xa_near, gate_far, qkv_w), up_far = after((ffn_own, xa_near, gate_far, qkv_w), up_far)
 
     segment = segment_ids[0]
     total_rows = segment.shape[0]
@@ -695,16 +695,15 @@
     d_qkv = attend_back_call(
         first, place.astype(jnp.int32), qkv, context, d_context, start, log_total, head
     )
-    ffn_0 = add_swapped(keep_0, send_0, "c", 1).astype(BF16)
     up_1 = add_swapped(*halves(ffn_1[1]), "y", 1).astype(BF16)
     gate_part = swap(gate_1, "zh", 1)
     ffn_out = [out_0, swap(out_1, NEAR, 1), swap(out_2, NEAR, 2)]
-    (ffn_1, out_3, out_grad), d_qkv, ffn_0, up_1, gate_part, *ffn_out = after(
-        (ffn_1, out_3, out_grad), d_qkv, ffn_0, up_1, gate_part, *ffn_out
+    (ffn_1, out_3, out_grad, keep_0), d_qkv, up_1, gate_part, *ffn_out = after(
+        (ffn_1, out_3, out_grad, keep_0), d_qkv, up_1, gate_part, *ffn_out
     )
 
     got = swap(d_qkv[:4], "zh", 1)
-    ffn_0 = add_swapped(*halves(ffn_0), "y", 1)
+    ffn_0 = add_swapped(keep_0, send_0, "c", 1).astype(BF16)
     out_grad = out_grad.reshape((4, 2) + out_grad.shape[1:])
     out_grad = out_grad[0].astype(F32) + sum(
         swap(out_grad[bit], NEAR, bit).astype(F32) for bit in (1, 2, 3)
@@ -718,20 +717,25 @@
     *d_xa, qkv_keep, qkv_send, head_parts, attn_gain_part = qkv_back_call(
         (d_qkv[4:], got), xa_near, qkv_w, cosine, sine, gains, head
     )
+    out_grad = add_swapped(*halves(out_grad), "y", 1)
     down_1 = add_swapped(*halves(ffn_1[2]), "y", 1).astype(BF16)
-    out_grad = add_swapped(*halves(out_grad), "y", 1)
     up_down = jnp.stack([up_1, down_1])
-    (up_down, out_3), d_xa, qkv_send, out_grad, attn_gain_part = after(
-        (up_down, out_3), d_xa, qkv_send, out_grad, attn_gain_part
+    (up_down, ffn_0, out_3), d_xa, qkv_send, out_grad, attn_gain_part = after(
+        (up_down, ffn_0, out_3), d_xa, qkv_send, out_grad, attn_gain_part
     )
 
     d_xa = [d_xa[0]] + [swap(d_xa[bit], NEAR, bit) for bit in (1, 2, 3)]
     qkv_grad = add_swapped(qkv_keep, qkv_send, "c", 1).astype(BF16)
+    qkv_grad = add_swapped(*halves(qkv_grad), "y", 1)
     up_down = swap(up_down, "zh", 1)
-    (qkv_grad, out_grad, out_3, attn_gain_part), d_xa, up_down = after(
-        (qkv_grad, out_grad, out_3, attn_gain_part), d_xa, up_down
-    )
-
+    ffn_0 = add_swapped(*halves(ffn_0), "y", 1)
+    (out_grad, out_3, attn_gain_part), d_xa, up_down, qkv_grad, ffn_0 = after(
+        (out_grad, out_3, attn_gain_part), d_xa, up_down, qkv_grad, ffn_0
+    )
+
+    heads_grad = jnp.concatenate([qkv_grad, out_grad], axis=1)
+    heads_grad = add_swapped(heads_grad[0], heads_grad[1].astype(BF16), "zh", 1)
+    qkv_grad, out_grad = heads_grad[:n], heads_grad[n:]
     ffn_out.append(swap(out_3, NEAR, 3))
     d = x.shape[1]
     gains = total_of(
@@ -744,11 +748,6 @@
             ]
         ).reshape(-1, 128)
     ).reshape(-1)
-    own, far = halves(qkv_grad)
-    qkv_grad = own[0].astype(F32) + swap(far[0], "y", 1).astype(F32)
-    qkv_grad = qkv_grad + swap(own[1], "zh", 1).astype(F32)
-    qkv_grad = qkv_grad + swap(far[1], ("y", "zh"), 3).astype(F32)
-    out_grad = add_swapped(out_grad[0], out_grad[1].astype(BF16), "zh", 1)
     d_xa = sum(v.astype(F32) for v in d_xa)
     x_back, _ = norm_back(x, x_factor, gain_a, d_xa)
     input_grad = arrays_order((d_hidden + x_back).astype(BF16), y, c)

time: 395 us -> 381 us (0.965)
  the two profiles are of different devices: /device:TPU:0 before, /device:TPU:8 now
where the time goes in v1:
time: 381 us; the launch traced here: 374 us
  waiting for transfers between devices  132 us (35%)
  Pallas kernels  89.6 us (24%)
  starting transfers between devices  77.9 us (20%)
  local copies, waits for them, and re-layouts  42 us (11%)
  other arithmetic  29.5 us (8%)
    ppermute x59, waiting for transfers between devices, swap(): return lax.ppermute(v, axes, [(i, i ^ bit) for i in range(size)])  132 us
    ppermute x59, starting transfers between devices, swap(): return lax.ppermute(v, axes, [(i, i ^ bit) for i in range(size)])  61.6 us
    unnamed x213, local copies, waits for them, and re-layouts  30.1 us
    pallas_call x3, Pallas kernels, ffn_call(): pl.pallas_call(functools.partial(ffn_kernel, count), out_shape=[jax.Shape...  26.8 us
    pallas_call x1, Pallas kernels, attend_back_call(): pl.pallas_call(functools.partial(attend_back_kernel, head), grid_spec=plt...  15.7 us
    pallas_call x2, Pallas kernels, ffn_grad_call(): pl.pallas_call(ffn_grad_kernel, grid=(three,), in_specs=[by_kind] * 4 + [...  14.2 us
    pallas_call x1, Pallas kernels, attend_call(): pl.pallas_call(functools.partial(attend_kernel, head), grid_spec=pltpu.Pr...  12.2 us
    all_to_all x2, starting transfers between devices, to_heads(): return lax.all_to_all(v, TENSOR, 0, 0, tiled=True)  10.5 us
  transfers between devices with their start and end apart: 62, of which 26 were waited for; matrix products, arithmetic and copies ran while one was open for 10% of the time, Pallas kernels for 23%

profile of v1, /device:TPU:8, one launch (start us, length us, event | category | flops | bytes accessed | tf_op | source)
XLA Modules:
  0.0 373.9 jit_solution(18238978529515516505)
XLA Ops:
  2.5 2.7 collective-permute-start.3
  15.1 5.2 %collective-permute-done.5 = bf16[384,256]{1,0:T(8,128)(2,1)S(1)} collective-permute-done((bf16[384,256]{1,0:T(8,128)(2,1)S(1)}, bf16[384,256]{1,0:T(8,128)(2,1)S(1)}, u32[]{:S(2)}, u32[]{:S(2)}) %collective-permute-start.5) | collective-permute-done | bytes 196640 | tf_op jit(solution)/shard_map/ppermute | solution.py:41
  24.2 3.6 collective-permute-done.2.refs_6_.refs_8_
  27.8 2.0 collective-permute-done.1.refs_2_.refs_4_
  31.4 3.8 %collective-permute-start.8 = (bf16[576,256]{1,0:T(8,128)(2,1)S(1)}, bf16[576,256]{1,0:T(8,128)(2,1)S(1)}, u32[]{:S(2)}, u32[]{:S(2)}) collective-permute-start(bf16[576,256]{1,0:T(8,128)(2,1)S(1)} %slice_bitcast_fusion.5), channel_id=1, source_target_pairs={{0,4},{4,0},{1,5},{5,1},{2,6},{6,2},{3,7},{7,3},{8,12},{12,8},{9,1... | collective-permute-start | bytes 884744 | tf_op jit(solution)/shard_map/ppermute | solution.py:41
  35.2 1.8 fusion.15
  38.1 8.1 %collective-permute-done.8.refs_10_.refs_12_ = bf16[576,256]{1,0:T(8,128)(2,1)S(1)} collective-permute-done((bf16[576,256]{1,0:T(8,128)(2,1)S(1)}, bf16[576,256]{1,0:T(8,128)(2,1)S(1)}, u32[]{:S(2)}, u32[]{:S(2)}) %collective-permute-start.8) | collective-permute-done | bytes 294944 | tf_op jit(solution)/shard_map/ppermute | solution.py:41
  46.9 4.2 %qkv.2 = bf16[4,256,256]{2,1,0:T(8,128)(2,1)} custom-call(bf16[256,1024]{1,0:T(8,128)(2,1)S(1)} %multiply_convert_fusion.refs_0_.refs_2_, bf16[256,1024]{1,0:T(8,128)(2,1)S(1)} %copy-done.21, bf16[256,1024]{1,0:T(8,128)(2,1)S(1)} %collective-permute-done.1.refs_2_.refs_4_, bf16[256,1024]{1,0:T(8,128)(2,1)S(1)} %collective-permute-done.7.refs_3_.refs_5_, ...), custom_call_target="tpu_custom_call" | custom-call | tf_op jit(solution)/shard_map/qkv/pallas_call | solution.py:154
  51.3 2.9 collective-permute-start.10
  61.0 3.2 qkv.3.refs_0_
  64.2 11.5 %collective-permute-done.10.refs_3_.refs_10_ = bf16[256,1024]{1,0:T(8,128)(2,1)} collective-permute-done((bf16[256,1024]{1,0:T(8,128)(2,1)S(1)}, bf16[256,1024]{1,0:T(8,128)(2,1)}, u32[]{:S(2)}, u32[]{:S(2)}) %collective-permute-start.10) | collective-permute-done | bytes 524320 | tf_op jit(solution)/shard_map/ppermute | solution.py:41
  75.7 2.6 collective-permute-done.11.refs_1_
  78.4 3.6 collective-permute-start.17
  83.3 2.4 collective-permute-start.13
  85.7 1.7 collective-permute-start.14
  89.4 12.2 %attend.1 = (bf16[2048,128]{1,0:T(8,128)(2,1)S(1)}, f32[8,1,512]{2,1,0:T(1,128)S(1)}, bf16[2048,256]{1,0:T(8,128)(2,1)S(1)}) custom-call(s32[8]{0:T(128)S(1)} %and_select_fusion.2.first, s32[8]{0:T(128)S(1)} %pad_add_fusion.1.at, bf16[4,256,256]{2,1,0:T(8,128)(2,1)S(1)} %copy-done.42, bf16[4,256,256]{2,1,0:T(8,128)(2,1)} %collective-permute-done.11.refs_1_, ...), custom_call_target="tpu_custom_call" | custom-call | tf_op jit(solution)/shard_map/attend/pallas_call | solution.py:217
  106.3 5.1 %all-to-all-start = ((bf16[8,256,128]{2,1,0:T(8,128)(2,1)}), bf16[8,256,128]{2,1,0:T(8,128)(2,1)}, u32[]{:S(2)}, u32[]{:S(2)}) async-start(bf16[8,256,128]{2,1,0:T(8,128)(2,1)} %bitcast.91), calls=%async_computation | async-start | bytes 1048576 | tf_op jit(solution)/shard_map/all_to_all | solution.py:652
  113.5 7.8 %collective-permute-done.18.refs_12_.refs_14_ = bf16[576,256]{1,0:T(8,128)(2,1)} collective-permute-done((bf16[576,256]{1,0:T(8,128)(2,1)}, bf16[576,256]{1,0:T(8,128)(2,1)}, u32[]{:S(2)}, u32[]{:S(2)}) %collective-permute-start.18) | collective-permute-done | bytes 294944 | tf_op jit(solution)/shard_map/ppermute | solution.py:41
  121.6 2.2 fusion.12.x
  123.7 5.9 %collective-permute-done.19.refs_16_.refs_18_ = bf16[576,256]{1,0:T(8,128)(2,1)S(1)} collective-permute-done((bf16[576,256]{1,0:T(8,128)(2,1)}, bf16[576,256]{1,0:T(8,128)(2,1)S(1)}, u32[]{:S(2)}, u32[]{:S(2)}) %collective-permute-start.19) | collective-permute-done | bytes 294944 | tf_op jit(solution)/shard_map/ppermute | solution.py:41
  136.7 2.4 project.1
  144.7 10.2 %collective-permute-done.32.refs_0_.refs_7_ = bf16[256,1024]{1,0:T(8,128)(2,1)S(1)} collective-permute-done((bf16[256,1024]{1,0:T(8,128)(2,1)S(1)}, bf16[256,1024]{1,0:T(8,128)(2,1)S(1)}, u32[]{:S(2)}, u32[]{:S(2)}) %collective-permute-start.32) | collective-permute-done | bytes 524320 | tf_op jit(solution)/shard_map/ppermute | solution.py:41
  155.0 6.7 %ffn.5 = (bf16[3,2,256,576]{3,2,1,0:T(8,128)(2,1)S(1)}, bf16[256,1024]{1,0:T(8,128)(2,1)S(1)}, bf16[256,1024]{1,0:T(8,128)(2,1)S(1)}) custom-call(bf16[256,1024]{1,0:T(8,128)(2,1)S(1)} %collective-permute-done.32.refs_0_.refs_7_, bf16[256,1024]{1,0:T(8,128)(2,1)S(1)} %copy-done.14, bf16[3,576,256]{2,1,0:T(8,128)(2,1)S(1)} %pad_maximum_fusion.1.refs_2_.refs_4_, ...), custom_call_target="tpu_custom_call" | custom-call | tf_op jit(solution)/shard_map/ffn/pallas_call | solution.py:512
  165.2 13.4 %ffn.4 = (bf16[3,2,256,576]{3,2,1,0:T(8,128)(2,1)S(1)}, bf16[256,1024]{1,0:T(8,128)(2,1)}, bf16[256,1024]{1,0:T(8,128)(2,1)S(1)}, bf16[3,2,256,576]{3,2,1,0:T(8,...) custom-call(bf16[256,1024]{1,0:T(8,128)(2,1)S(1)} %collective-permute-done.30.refs_0_.refs_5_, ...), custom_call_target="tpu_custom_call" | custom-call | tf_op jit(solution)/shard_map/ffn/pallas_call | solution.py:512
  181.5 6.7 %ffn.3 = (bf16[3,2,256,576]{3,2,1,0:T(8,128)(2,1)S(1)}, bf16[256,1024]{1,0:T(8,128)(2,1)S(1)}, bf16[256,1024]{1,0:T(8,128)(2,1)S(1)}) custom-call(bf16[256,1024]{1,0:T(8,128)(2,1)S(1)} %get-tuple-element.216.refs_0_.refs_4_, bf16[256,1024]{1,0:T(8,128)(2,1)S(1)} %pad_maximum_fusion.7.refs_1_.refs_8_.dy, ...), custom_call_target="tpu_custom_call" | custom-call | tf_op jit(solution)/shard_map/ffn/pallas_call | solution.py:512
  189.0 6.5 %ffn_grad.3 = (bf16[3,576,512]{2,1,0:T(8,128)(2,1)S(1)}, bf16[3,576,512]{2,1,0:T(8,128)(2,1)S(1)}) custom-call(bf16[3,2,256,576]{3,2,1,0:T(8,128)(2,1)S(1)} %get-tuple-element.239.refs_0_, bf16[3,2,256,576]{3,2,1,0:T(8,128)(2,1)S(1)} %get-tuple-element.240.refs_1_, bf16[3,2,256,576]{3,2,1,0:T(8,128)(2,1)S(1)} %copy-done.12, ...), custom_call_target="tpu_custom_call" | custom-call | tf_op jit(solution)/shard_map/ffn_grad/pallas_call | solution.py:543
  198.0 7.7 %ffn_grad.2 = (bf16[3,576,512]{2,1,0:T(8,128)(2,1)S(1)}, bf16[3,576,512]{2,1,0:T(8,128)(2,1)}) custom-call(bf16[3,2,256,576]{3,2,1,0:T(8,128)(2,1)S(1)} %get-tuple-element.239.refs_0_, bf16[3,2,256,576]{3,2,1,0:T(8,128)(2,1)S(1)} %get-tuple-element.240.refs_1_, bf16[3,2,256,576]{3,2,1,0:T(8,128)(2,1)S(1)} %copy-done.12, bf16[3,2,256,576]{3,2,1,0:T(8,128)(2,1)} %copy-done.11, ...), custom_call_target="tpu_custom_call" | custom-call | tf_op jit(solution)/shard_map/ffn_grad/pallas_call | solution.py:543
  207.1 4.2 %project_back.1 = (bf16[8,256,128]{2,1,0:T(8,128)(2,1)S(1)}, bf16[8,128,512]{2,1,0:T(8,128)(2,1)S(1)}, bf16[8,128,512]{2,1,0:T(8,128)(2,1)}, f32[256,1024]{1,0:T(8,128)S(1)}, f32[1,1024]{1,0:T(1,128)S(1)}) custom-call(s32[8]{0:T(128)S(1)} %copy-done.67, bf16[8,256,128]{2,1,0:T(8,128)(2,1)} %all-to-all-done.context, bf16[8,128,512]{2,1,0:T(8,128)(2,1)S(1)} %bitcast.90, ...), custom_call_target="tpu_custom_call" | custom-call | tf_op jit(solution)/shard_map/project_back/pallas_call | solution.py:404
  214.6 5.4 %all-to-all-start.1 = ((bf16[8,256,128]{2,1,0:T(8,128)(2,1)}), bf16[8,256,128]{2,1,0:T(8,128)(2,1)S(1)}, u32[]{:S(2)}, u32[]{:S(2)}) async-start(bf16[8,256,128]{2,1,0:T(8,128)(2,1)} %copy-done.54), calls=%async_computation.1 | async-start | bytes 1048576 | tf_op jit(solution)/shard_map/all_to_all | solution.py:652
  220.0 2.5 add_convert_fusion.1
  224.4 2.5 add_convert_fusion.2
  226.9 5.2 %collective-permute-done.37 = bf16[576,256]{1,0:T(8,128)(2,1)S(1)} collective-permute-done((bf16[576,256]{1,0:T(8,128)(2,1)S(1)}, bf16[576,256]{1,0:T(8,128)(2,1)S(1)}, u32[]{:S(2)}, u32[]{:S(2)}) %collective-permute-start.37) | collective-permute-done | bytes 294944 | tf_op jit(solution)/shard_map/ppermute | solution.py:41
  236.1 1.8 collective-permute-start.42
  240.3 15.7 %attend_back.1 = bf16[8,256,256]{2,1,0:T(8,128)(2,1)S(1)} custom-call(s32[8]{0:T(128)S(1)} %copy-done.71, s32[8]{0:T(128)S(1)} %fusion.7.to, bf16[2048,256]{1,0:T(8,128)(2,1)S(1)} %copy-done.51, bf16[2048,128]{1,0:T(8,128)(2,1)S(1)} %copy-done.40, bf16[2048,128]{1,0:T(8,128)(2,1)S(1)} %bitcast.92, s32[8,1,512]{2,1,0:T(1,128)S(1)} %pad_add_fusion.refs_2_.start, ...), custom_call_target="tpu_custom_call" | custom-call | tf_op jit(solution)/shard_map/attend_back/pallas_call | solution.py:306
  256.4 1.7 collective-permute-start.43
  261.7 2.0 add_convert_fusion
  264.6 12.6 %collective-permute-done.47 = bf16[2,128,512]{2,1,0:T(8,128)(2,1)S(1)} collective-permute-done((bf16[2,128,512]{2,1,0:T(8,128)(2,1)S(1)}, bf16[2,128,512]{2,1,0:T(8,128)(2,1)S(1)}, u32[]{:S(2)}, u32[]{:S(2)}) %collective-permute-start.47) | collective-permute-done | bytes 262176 | tf_op jit(solution)/shard_map/ppermute | solution.py:41
  277.2 3.3 collective-permute-done.46
  284.3 6.7 %qkv_back.1 = (bf16[256,1024]{1,0:T(8,128)(2,1)S(1)}, bf16[256,1024]{1,0:T(8,128)(2,1)S(1)}, bf16[256,1024]{1,0:T(8,128)(2,1)S(1)}, bf16[256,1024]{1,0:T(8,128)(...) custom-call(bf16[4,256,256]{2,1,0:T(8,128)(2,1)S(1)} %slice.147.refs, ...), custom_call_target="tpu_custom_call" | custom-call | tf_op jit(solution)/shard_map/qkv_back/pallas_call | solution.py:466
  294.7 3.4 collective-permute-start.53
  298.7 20.9 %collective-permute-done.55 = bf16[2,256,256]{2,1,0:T(8,128)(2,1)S(1)} collective-permute-done((bf16[2,256,256]{2,1,0:T(8,128)(2,1)S(1)}, bf16[2,256,256]{2,1,0:T(8,128)(2,1)S(1)}, u32[]{:S(2)}, u32[]{:S(2)}) %collective-permute-start.55) | collective-permute-done | bytes 262176 | tf_op jit(solution)/shard_map/ppermute | solution.py:41
  319.6 2.6 collective-permute-start.52
  323.7 10.6 %collective-permute-done.52 = bf16[256,1024]{1,0:T(8,128)(2,1)S(1)} collective-permute-done((bf16[256,1024]{1,0:T(8,128)(2,1)S(1)}, bf16[256,1024]{1,0:T(8,128)(2,1)S(1)}, u32[]{:S(2)}, u32[]{:S(2)}) %collective-permute-start.52) | collective-permute-done | bytes 524320 | tf_op jit(solution)/shard_map/ppermute | solution.py:41
  336.3 5.8 %all-to-all-start.2 = ((f32[32,17,128]{2,1,0:T(8,128)}), f32[32,17,128]{2,1,0:T(8,128)S(1)}, u32[]{:S(2)}, u32[]{:S(2)}) async-start(f32[32,17,128]{2,1,0:T(8,128)} %broadcast_in_dim.38), calls=%async_computation.2 | async-start | bytes 786432 | tf_op jit(solution)/shard_map/all_to_all | solution.py:88
  343.7 2.4 collective-permute-start.58
  346.2 2.4 add_bitcast_fusion
  349.4 2.1 fusion
  351.5 16.1 %collective-permute-done.58 = bf16[384,256]{1,0:T(8,128)(2,1)S(1)} collective-permute-done((bf16[384,256]{1,0:T(8,128)(2,1)S(1)}, bf16[384,256]{1,0:T(8,128)(2,1)S(1)}, u32[]{:S(2)}, u32[]{:S(2)}) %collective-permute-start.58) | collective-permute-done | bytes 196640 | tf_op jit(solution)/shard_map/ppermute | solution.py:41
  (397 shorter events, 95.6 us)
Async XLA Ops:
  2.5 11.1 %collective-permute-start.3 = (bf16[384,256]{1,0:T(8,128)(2,1)S(1)}, bf16[384,256]{1,0:T(8,128)(2,1)S(1)}, u32[]{:S(2)}, u32[]{:S(2)}) collective-permute-start(bf16[384,256]{1,0:T(8,128)(2,1)S(1)} %get-tuple-element.401), channel_id=1, source_target_pairs={{0,4},{4,0},{1,5},{5,1},{2,6},{6,2},{3,7},{7,3},{8,12},{12,8},{9,1... | collective-permute-start | bytes 589832 | tf_op jit(solution)/shard_map/ppermute | solution.py:41
  5.1 10.0 %collective-permute-start.4 = (bf16[384,256]{1,0:T(8,128)(2,1)S(1)}, bf16[384,256]{1,0:T(8,128)(2,1)S(1)}, u32[]{:S(2)}, u32[]{:S(2)}) collective-permute-start(bf16[384,256]{1,0:T(8,128)(2,1)S(1)} %get-tuple-element.401), channel_id=1, source_target_pairs={{0,16},{16,0},{1,17},{17,1},{2,18},{18,2},{3,19},{19,3},{4,20},{20... | collective-permute-start | bytes 589832 | tf_op jit(solution)/shard_map/ppermute | solution.py:41
  9.5 20.2 %collective-permute-start.1 = (bf16[256,1024]{1,0:T(8,128)(2,1)S(1)}, bf16[256,1024]{1,0:T(8,128)(2,1)S(1)}, u32[]{:S(2)}, u32[]{:S(2)}) collective-permute-start(bf16[256,1024]{1,0:T(8,128)(2,1)S(1)} %multiply_convert_fusion.refs_0_.refs_2_), channel_id=1, source_target_pairs={{0,2},{1,3},{2,0},{3,1},{4,6},{5,7},{6,4},{7,5},{8,10},{9,11},{10,... | collective-permute-start | bytes 1572872 | tf_op jit(solution)/shard_map/ppermute | solution.py:41
  10.1 19.7 %collective-permute-start = (bf16[256,1024]{1,0:T(8,128)(2,1)S(1)}, bf16[256,1024]{1,0:T(8,128)(2,1)S(1)}, u32[]{:S(2)}, u32[]{:S(2)}) collective-permute-start(bf16[256,1024]{1,0:T(8,128)(2,1)S(1)} %multiply_convert_fusion.refs_0_.refs_2_), channel_id=1, source_target_pairs={{0,1},{1,0},{2,3},{3,2},{4,5},{5,4},{6,7},{7,6},{8,9},{9,8},{10,11... | collective-permute-start | bytes 1572872 | tf_op jit(solution)/shard_map/ppermute | solution.py:41
  11.6 16.3 %collective-permute-start.2 = (bf16[576,256]{1,0:T(8,128)(2,1)}, bf16[576,256]{1,0:T(8,128)(2,1)S(1)}, u32[]{:S(2)}, u32[]{:S(2)}) collective-permute-start(bf16[576,256]{1,0:T(8,128)(2,1)} %bitcast.2), channel_id=1, source_target_pairs={{0,4},{4,0},{1,5},{5,1},{2,6},{6,2},{3,7},{7,3},{8,12},{12,8},{9,1... | collective-permute-start | bytes 884744 | tf_op jit(solution)/shard_map/ppermute | solution.py:41
  29.8 16.4 %collective-permute-start.7 = (bf16[256,1024]{1,0:T(8,128)(2,1)S(1)}, bf16[256,1024]{1,0:T(8,128)(2,1)S(1)}, u32[]{:S(2)}, u32[]{:S(2)}) collective-permute-start(bf16[256,1024]{1,0:T(8,128)(2,1)S(1)} %collective-permute-done.1.refs_2_.refs_4_), channel_id=1, source_target_pairs={{0,1},{1,0},{2,3},{3,2},{4,5},{5,4},{6,7},{7,6},{8,9},{9,8},{10,11... | collective-permute-start | bytes 1572872 | tf_op jit(solution)/shard_map/ppermute | solution.py:41
  31.4 14.8 %collective-permute-start.8 = (bf16[576,256]{1,0:T(8,128)(2,1)S(1)}, bf16[576,256]{1,0:T(8,128)(2,1)S(1)}, u32[]{:S(2)}, u32[]{:S(2)}) collective-permute-start(bf16[576,256]{1,0:T(8,128)(2,1)S(1)} %slice_bitcast_fusion.5), channel_id=1, source_target_pairs={{0,4},{4,0},{1,5},{5,1},{2,6},{6,2},{3,7},{7,3},{8,12},{12,8},{9,1... | collective-permute-start | bytes 884744 | tf_op jit(solution)/shard_map/ppermute | solution.py:41
  51.1 27.2 %collective-permute-start.12 = (bf16[3,576,256]{2,1,0:T(8,128)(2,1)S(1)}, bf16[3,576,256]{2,1,0:T(8,128)(2,1)}, u32[]{:S(2)}, u32[]{:S(2)}) collective-permute-start(bf16[3,576,256]{2,1,0:T(8,128)(2,1)S(1)} %pad_maximum_fusion.1.refs_2_.refs_4_), channel_id=1, source_target_pairs={{0,16},{16,0},{1,17},{17,1},{2,18},{18,2},{3,19},{19,3},{4,20},{20... | collective-permute-start | bytes 2654216 | tf_op jit(solution)/shard_map/ppermute | solution.py:41
  51.3 24.4 %collective-permute-start.10 = (bf16[256,1024]{1,0:T(8,128)(2,1)S(1)}, bf16[256,1024]{1,0:T(8,128)(2,1)}, u32[]{:S(2)}, u32[]{:S(2)}) collective-permute-start(bf16[256,1024]{1,0:T(8,128)(2,1)S(1)} %pad_maximum_fusion.7.refs_1_.refs_8_.dy), channel_id=1, source_target_pairs={{0,2},{1,3},{2,0},{3,1},{4,6},{5,7},{6,4},{7,5},{8,10},{9,11},{10,... | collective-permute-start | bytes 1572872 | tf_op jit(solution)/shard_map/ppermute | solution.py:41
  54.2 21.5 %collective-permute-start.9 = (bf16[256,1024]{1,0:T(8,128)(2,1)S(1)}, bf16[256,1024]{1,0:T(8,128)(2,1)}, u32[]{:S(2)}, u32[]{:S(2)}) collective-permute-start(bf16[256,1024]{1,0:T(8,128)(2,1)S(1)} %pad_maximum_fusion.7.refs_1_.refs_8_.dy), channel_id=1, source_target_pairs={{0,1},{1,0},{2,3},{3,2},{4,5},{5,4},{6,7},{7,6},{8,9},{9,8},{10,11... | collective-permute-start | bytes 1572872 | tf_op jit(solution)/shard_map/ppermute | solution.py:41
  54.7 23.6 %collective-permute-start.11 = (bf16[4,256,256]{2,1,0:T(8,128)(2,1)}, bf16[4,256,256]{2,1,0:T(8,128)(2,1)}, u32[]{:S(2)}, u32[]{:S(2)}) collective-permute-start(bf16[4,256,256]{2,1,0:T(8,128)(2,1)} %qkv.2), channel_id=1, source_target_pairs={{0,4},{4,0},{1,5},{5,1},{2,6},{6,2},{3,7},{7,3},{8,12},{12,8},{9,1... | collective-permute-start | bytes 1572872 | tf_op jit(solution)/shard_map/ppermute | solution.py:41
  78.4 25.6 %collective-permute-start.17 = (bf16[2,128,512]{2,1,0:T(8,128)(2,1)S(1)}, bf16[2,128,512]{2,1,0:T(8,128)(2,1)}, u32[]{:S(2)}, u32[]{:S(2)}) collective-permute-start(bf16[2,128,512]{2,1,0:T(8,128)(2,1)S(1)} %pad_maximum_fusion.10), channel_id=1, source_target_pairs={{0,3},{1,2},{2,1},{3,0},{4,7},{5,6},{6,5},{7,4},{8,11},{9,10},{10,... | collective-permute-start | bytes 786440 | tf_op jit(solution)/shard_map/ppermute | solution.py:41
  82.0 22.1 %collective-permute-start.16 = (bf16[2,128,512]{2,1,0:T(8,128)(2,1)S(1)}, bf16[2,128,512]{2,1,0:T(8,128)(2,1)}, u32[]{:S(2)}, u32[]{:S(2)}) collective-permute-start(bf16[2,128,512]{2,1,0:T(8,128)(2,1)S(1)} %pad_maximum_fusion.10), channel_id=1, source_target_pairs={{0,2},{1,3},{2,0},{3,1},{4,6},{5,7},{6,4},{7,5},{8,10},{9,11},{10,... | collective-permute-start | bytes 786440 | tf_op jit(solution)/shard_map/ppermute | solution.py:41
  82.0 22.1 %collective-permute-start.15 = (bf16[2,128,512]{2,1,0:T(8,128)(2,1)S(1)}, bf16[2,128,512]{2,1,0:T(8,128)(2,1)}, u32[]{:S(2)}, u32[]{:S(2)}) collective-permute-start(bf16[2,128,512]{2,1,0:T(8,128)(2,1)S(1)} %pad_maximum_fusion.10), channel_id=1, source_target_pairs={{0,1},{1,0},{2,3},{3,2},{4,5},{5,4},{6,7},{7,6},{8,9},{9,8},{10,11... | collective-permute-start | bytes 786440 | tf_op jit(solution)/shard_map/ppermute | solution.py:41
  83.3 20.7 %collective-permute-start.13 = (bf16[576,256]{1,0:T(8,128)(2,1)}, bf16[576,256]{1,0:T(8,128)(2,1)S(1)}, u32[]{:S(2)}, u32[]{:S(2)}) collective-permute-start(bf16[576,256]{1,0:T(8,128)(2,1)} %slice_bitcast_fusion.4), channel_id=1, source_target_pairs={{0,4},{4,0},{1,5},{5,1},{2,6},{6,2},{3,7},{7,3},{8,12},{12,8},{9,1... | collective-permute-start | bytes 884744 | tf_op jit(solution)/shard_map/ppermute | solution.py:41
  85.7 18.3 %collective-permute-start.14 = (bf16[576,256]{1,0:T(8,128)(2,1)S(1)}, bf16[576,256]{1,0:T(8,128)(2,1)S(1)}, u32[]{:S(2)}, u32[]{:S(2)}) collective-permute-start(bf16[576,256]{1,0:T(8,128)(2,1)S(1)} %collective-permute-done.2.refs_6_.refs_8_), channel_id=1, source_target_pairs={{0,16},{16,0},{1,17},{17,1},{2,18},{18,2},{3,19},{19,3},{4,20},{20... | collective-permute-start | bytes 884744 | tf_op jit(solution)/shard_map/ppermute | solution.py:41
  106.2 26.9 %collective-permute-start.23 = (bf16[4,2,128,512]{3,2,1,0:T(8,128)(2,1)S(1)}, bf16[4,2,128,512]{3,2,1,0:T(8,128)(2,1)}, u32[]{:S(2)}, u32[]{:S(2)}) collective-permute-start(bf16[4,2,128,512]{3,2,1,0:T(8,128)(2,1)S(1)} %pad_maximum_fusion), channel_id=1, source_target_pairs={{0,8},{8,0},{1,9},{9,1},{2,10},{10,2},{3,11},{11,3},{4,12},{12,4},... | collective-permute-start | bytes 3145736 | tf_op jit(solution)/shard_map/ppermute | solution.py:41
  106.3 26.8 %all-to-all-start = ((bf16[8,256,128]{2,1,0:T(8,128)(2,1)}), bf16[8,256,128]{2,1,0:T(8,128)(2,1)}, u32[]{:S(2)}, u32[]{:S(2)}) async-start(bf16[8,256,128]{2,1,0:T(8,128)(2,1)} %bitcast.91), calls=%async_computation | async-start | bytes 1048576 | tf_op jit(solution)/shard_map/all_to_all | solution.py:652
  111.4 19.7 %collective-permute-start.21 = (bf16[3,576,256]{2,1,0:T(8,128)(2,1)S(1)}, bf16[3,576,256]{2,1,0:T(8,128)(2,1)S(1)}, u32[]{:S(2)}, u32[]{:S(2)}) collective-permute-start(bf16[3,576,256]{2,1,0:T(8,128)(2,1)S(1)} %pad_maximum_fusion.1.refs_2_.refs_4_), channel_id=1, source_target_pairs={{0,8},{8,0},{1,9},{9,1},{2,10},{10,2},{3,11},{11,3},{4,12},{12,4},... | collective-permute-start | bytes 2654216 | tf_op jit(solution)/shard_map/ppermute | solution.py:41
  111.5 20.6 %collective-permute-start.22 = (bf16[3,576,256]{2,1,0:T(8,128)(2,1)}, bf16[3,576,256]{2,1,0:T(8,128)(2,1)S(1)}, u32[]{:S(2)}, u32[]{:S(2)}) collective-permute-start(bf16[3,576,256]{2,1,0:T(8,128)(2,1)} %collective-permute-done.12.refs_4_.refs_6_), channel_id=1, source_target_pairs={{0,8},{8,0},{1,9},{9,1},{2,10},{10,2},{3,11},{11,3},{4,12},{12,4},... | collective-permute-start | bytes 2654216 | tf_op jit(solution)/shard_map/ppermute | solution.py:41
  112.0 18.3 %collective-permute-start.20 = (bf16[256,1024]{1,0:T(8,128)(2,1)}, bf16[256,1024]{1,0:T(8,128)(2,1)S(1)}, u32[]{:S(2)}, u32[]{:S(2)}) collective-permute-start(bf16[256,1024]{1,0:T(8,128)(2,1)} %collective-permute-done.10.refs_3_.refs_10_), channel_id=1, source_target_pairs={{0,1},{1,0},{2,3},{3,2},{4,5},{5,4},{6,7},{7,6},{8,9},{9,8},{10,11... | collective-permute-start | bytes 1572872 | tf_op jit(solution)/shard_map/ppermute | solution.py:41
  139.1 15.8 %collective-permute-start.32 = (bf16[256,1024]{1,0:T(8,128)(2,1)S(1)}, bf16[256,1024]{1,0:T(8,128)(2,1)S(1)}, u32[]{:S(2)}, u32[]{:S(2)}) collective-permute-start(bf16[256,1024]{1,0:T(8,128)(2,1)S(1)} %get-tuple-element.216.refs_0_.refs_4_), channel_id=1, source_target_pairs={{0,3},{1,2},{2,1},{3,0},{4,7},{5,6},{6,5},{7,4},{8,11},{9,10},{10,... | collective-permute-start | bytes 1572872 | tf_op jit(solution)/shard_map/ppermute | solution.py:41
  140.1 24.6 %collective-permute-start.31 = (bf16[256,1024]{1,0:T(8,128)(2,1)S(1)}, bf16[256,1024]{1,0:T(8,128)(2,1)S(1)}, u32[]{:S(2)}, u32[]{:S(2)}) collective-permute-start(bf16[256,1024]{1,0:T(8,128)(2,1)S(1)} %get-tuple-element.216.refs_0_.refs_4_), channel_id=1, source_target_pairs={{0,2},{1,3},{2,0},{3,1},{4,6},{5,7},{6,4},{7,5},{8,10},{9,11},{10,... | collective-permute-start | bytes 1572872 | tf_op jit(solution)/shard_map/ppermute | solution.py:41
  141.6 23.7 %collective-permute-start.30 = (bf16[256,1024]{1,0:T(8,128)(2,1)S(1)}, bf16[256,1024]{1,0:T(8,128)(2,1)S(1)}, u32[]{:S(2)}, u32[]{:S(2)}) collective-permute-start(bf16[256,1024]{1,0:T(8,128)(2,1)S(1)} %get-tuple-element.216.refs_0_.refs_4_), channel_id=1, source_target_pairs={{0,1},{1,0},{2,3},{3,2},{4,5},{5,4},{6,7},{7,6},{8,9},{9,8},{10,11... | collective-permute-start | bytes 1572872 | tf_op jit(solution)/shard_map/ppermute | solution.py:41
  163.8 43.2 %collective-permute-start.35 = (bf16[256,1024]{1,0:T(8,128)(2,1)S(1)}, bf16[256,1024]{1,0:T(8,128)(2,1)S(1)}, u32[]{:S(2)}, u32[]{:S(2)}) collective-permute-start(bf16[256,1024]{1,0:T(8,128)(2,1)S(1)} %get-tuple-element.238), channel_id=1, source_target_pairs={{0,3},{1,2},{2,1},{3,0},{4,7},{5,6},{6,5},{7,4},{8,11},{9,10},{10,... | collective-permute-start | bytes 1572872 | tf_op jit(solution)/shard_map/ppermute | solution.py:41
  179.5 27.5 %collective-permute-start.33 = (bf16[256,1024]{1,0:T(8,128)(2,1)S(1)}, bf16[256,1024]{1,0:T(8,128)(2,1)S(1)}, u32[]{:S(2)}, u32[]{:S(2)}) collective-permute-start(bf16[256,1024]{1,0:T(8,128)(2,1)S(1)} %get-tuple-element.236), channel_id=1, source_target_pairs={{0,1},{1,0},{2,3},{3,2},{4,5},{5,4},{6,7},{7,6},{8,9},{9,8},{10,11... | collective-permute-start | bytes 1572872 | tf_op jit(solution)/shard_map/ppermute | solution.py:41
  180.4 26.6 %collective-permute-start.34 = (bf16[256,1024]{1,0:T(8,128)(2,1)S(1)}, bf16[256,1024]{1,0:T(8,128)(2,1)S(1)}, u32[]{:S(2)}, u32[]{:S(2)}) collective-permute-start(bf16[256,1024]{1,0:T(8,128)(2,1)S(1)} %get-tuple-element.237), channel_id=1, source_target_pairs={{0,2},{1,3},{2,0},{3,1},{4,6},{5,7},{6,4},{7,5},{8,10},{9,11},{10,... | collective-permute-start | bytes 1572872 | tf_op jit(solution)/shard_map/ppermute | solution.py:41
  207.0 13.0 %collective-permute-start.36 = (bf16[3,576,512]{2,1,0:T(8,128)(2,1)}, bf16[3,576,512]{2,1,0:T(8,128)(2,1)}, u32[]{:S(2)}, u32[]{:S(2)}) collective-permute-start(bf16[3,576,512]{2,1,0:T(8,128)(2,1)} %get-tuple-element.252), channel_id=1, source_target_pairs={{0,8},{8,0},{1,9},{9,1},{2,10},{10,2},{3,11},{11,3},{4,12},{12,4},... | collective-permute-start | bytes 5308424 | tf_op jit(solution)/shard_map/ppermute | solution.py:41
  214.6 18.8 %all-to-all-start.1 = ((bf16[8,256,128]{2,1,0:T(8,128)(2,1)}), bf16[8,256,128]{2,1,0:T(8,128)(2,1)S(1)}, u32[]{:S(2)}, u32[]{:S(2)}) async-start(bf16[8,256,128]{2,1,0:T(8,128)(2,1)} %copy-done.54), calls=%async_computation.1 | async-start | bytes 1048576 | tf_op jit(solution)/shard_map/all_to_all | solution.py:652
  220.0 41.7 %collective-permute-start.44 = (bf16[3,576,512]{2,1,0:T(8,128)(2,1)}, bf16[3,576,512]{2,1,0:T(8,128)(2,1)}, u32[]{:S(2)}, u32[]{:S(2)}) collective-permute-start(bf16[3,576,512]{2,1,0:T(8,128)(2,1)} %copy-done.72), channel_id=1, source_target_pairs={{0,8},{8,0},{1,9},{9,1},{2,10},{10,2},{3,11},{11,3},{4,12},{12,4},... | collective-permute-start | bytes 5308424 | tf_op jit(solution)/shard_map/ppermute | solution.py:41
  222.6 9.5 %collective-permute-start.37 = (bf16[576,256]{1,0:T(8,128)(2,1)S(1)}, bf16[576,256]{1,0:T(8,128)(2,1)S(1)}, u32[]{:S(2)}, u32[]{:S(2)}) collective-permute-start(bf16[576,256]{1,0:T(8,128)(2,1)S(1)} %split.185), channel_id=1, source_target_pairs={{0,16},{16,0},{1,17},{17,1},{2,18},{18,2},{3,19},{19,3},{4,20},{20... | collective-permute-start | bytes 884744 | tf_op jit(solution)/shard_map/ppermute | solution.py:41
  234.5 21.5 %collective-permute-start.39 = (bf16[576,256]{1,0:T(8,128)(2,1)S(1)}, bf16[576,256]{1,0:T(8,128)(2,1)S(1)}, u32[]{:S(2)}, u32[]{:S(2)}) collective-permute-start(bf16[576,256]{1,0:T(8,128)(2,1)S(1)} %split.187), channel_id=1, source_target_pairs={{0,16},{16,0},{1,17},{17,1},{2,18},{18,2},{3,19},{19,3},{4,20},{20... | collective-permute-start | bytes 884744 | tf_op jit(solution)/shard_map/ppermute | solution.py:41
  235.2 21.1 %collective-permute-start.41 = (bf16[256,1024]{1,0:T(8,128)(2,1)}, bf16[256,1024]{1,0:T(8,128)(2,1)S(1)}, u32[]{:S(2)}, u32[]{:S(2)}) collective-permute-start(bf16[256,1024]{1,0:T(8,128)(2,1)} %get-tuple-element.269), channel_id=1, source_target_pairs={{0,1},{1,0},{2,3},{3,2},{4,5},{5,4},{6,7},{7,6},{8,9},{9,8},{10,11... | collective-permute-start | bytes 1572872 | tf_op jit(solution)/shard_map/ppermute | solution.py:41
  236.1 20.2 %collective-permute-start.42 = (bf16[256,1024]{1,0:T(8,128)(2,1)S(1)}, bf16[256,1024]{1,0:T(8,128)(2,1)S(1)}, u32[]{:S(2)}, u32[]{:S(2)}) collective-permute-start(bf16[256,1024]{1,0:T(8,128)(2,1)S(1)} %copy-done.76), channel_id=1, source_target_pairs={{0,2},{1,3},{2,0},{3,1},{4,6},{5,7},{6,4},{7,5},{8,10},{9,11},{10,... | collective-permute-start | bytes 1572872 | tf_op jit(solution)/shard_map/ppermute | solution.py:41
  237.9 18.4 %collective-permute-start.40 = (bf16[576,256]{1,0:T(8,128)(2,1)}, bf16[576,256]{1,0:T(8,128)(2,1)S(1)}, u32[]{:S(2)}, u32[]{:S(2)}) collective-permute-start(bf16[576,256]{1,0:T(8,128)(2,1)} %add_convert_fusion.8), channel_id=1, source_target_pairs={{0,4},{4,0},{1,5},{5,1},{2,6},{6,2},{3,7},{7,3},{8,12},{12,8},{9,1... | collective-permute-start | bytes 884744 | tf_op jit(solution)/shard_map/ppermute | solution.py:41
  256.4 24.4 %collective-permute-start.43 = (bf16[4,256,256]{2,1,0:T(8,128)(2,1)S(1)}, bf16[4,256,256]{2,1,0:T(8,128)(2,1)S(1)}, u32[]{:S(2)}, u32[]{:S(2)}) collective-permute-start(bf16[4,256,256]{2,1,0:T(8,128)(2,1)S(1)} %slice.141), channel_id=1, source_target_pairs={{0,4},{4,0},{1,5},{5,1},{2,6},{6,2},{3,7},{7,3},{8,12},{12,8},{9,1... | collective-permute-start | bytes 1572872 | tf_op jit(solution)/shard_map/ppermute | solution.py:41
  258.8 18.4 %collective-permute-start.47 = (bf16[2,128,512]{2,1,0:T(8,128)(2,1)S(1)}, bf16[2,128,512]{2,1,0:T(8,128)(2,1)S(1)}, u32[]{:S(2)}, u32[]{:S(2)}) collective-permute-start(bf16[2,128,512]{2,1,0:T(8,128)(2,1)S(1)} %get-tuple-element.374), channel_id=1, source_target_pairs={{0,3},{1,2},{2,1},{3,0},{4,7},{5,6},{6,5},{7,4},{8,11},{9,10},{10,... | collective-permute-start | bytes 786440 | tf_op jit(solution)/shard_map/ppermute | solution.py:41
  260.1 20.4 %collective-permute-start.46 = (bf16[2,128,512]{2,1,0:T(8,128)(2,1)S(1)}, bf16[2,128,512]{2,1,0:T(8,128)(2,1)S(1)}, u32[]{:S(2)}, u32[]{:S(2)}) collective-permute-start(bf16[2,128,512]{2,1,0:T(8,128)(2,1)S(1)} %get-tuple-element.375), channel_id=1, source_target_pairs={{0,2},{1,3},{2,0},{3,1},{4,6},{5,7},{6,4},{7,5},{8,10},{9,11},{10,... | collective-permute-start | bytes 786440 | tf_op jit(solution)/shard_map/ppermute | solution.py:41
  280.8 10.2 %collective-permute-start.49 = (bf16[2,128,256]{2,1,0:T(8,128)(2,1)S(1)}, bf16[2,128,256]{2,1,0:T(8,128)(2,1)S(1)}, u32[]{:S(2)}, u32[]{:S(2)}) collective-permute-start(bf16[2,128,256]{2,1,0:T(8,128)(2,1)S(1)} %split.155), channel_id=1, source_target_pairs={{0,16},{16,0},{1,17},{17,1},{2,18},{18,2},{3,19},{19,3},{4,20},{20... | collective-permute-start | bytes 393224 | tf_op jit(solution)/shard_map/ppermute | solution.py:41
  291.9 30.4 %collective-permute-start.56 = (bf16[3,576,256]{2,1,0:T(8,128)(2,1)S(1)}, bf16[3,576,256]{2,1,0:T(8,128)(2,1)S(1)}, u32[]{:S(2)}, u32[]{:S(2)}) collective-permute-start(bf16[3,576,256]{2,1,0:T(8,128)(2,1)S(1)} %split.159), channel_id=1, source_target_pairs={{0,16},{16,0},{1,17},{17,1},{2,18},{18,2},{3,19},{19,3},{4,20},{20... | collective-permute-start | bytes 2654216 | tf_op jit(solution)/shard_map/ppermute | solution.py:41
  293.9 25.7 %collective-permute-start.55 = (bf16[2,256,256]{2,1,0:T(8,128)(2,1)S(1)}, bf16[2,256,256]{2,1,0:T(8,128)(2,1)S(1)}, u32[]{:S(2)}, u32[]{:S(2)}) collective-permute-start(bf16[2,256,256]{2,1,0:T(8,128)(2,1)S(1)} %split.191), channel_id=1, source_target_pairs={{0,16},{16,0},{1,17},{17,1},{2,18},{18,2},{3,19},{19,3},{4,20},{20... | collective-permute-start | bytes 786440 | tf_op jit(solution)/shard_map/ppermute | solution.py:41
  294.7 39.6 %collective-permute-start.53 = (bf16[2,576,256]{2,1,0:T(8,128)(2,1)S(1)}, bf16[2,576,256]{2,1,0:T(8,128)(2,1)S(1)}, u32[]{:S(2)}, u32[]{:S(2)}) collective-permute-start(bf16[2,576,256]{2,1,0:T(8,128)(2,1)S(1)} %pad_maximum_fusion.3), channel_id=1, source_target_pairs={{0,4},{4,0},{1,5},{5,1},{2,6},{6,2},{3,7},{7,3},{8,12},{12,8},{9,1... | collective-permute-start | bytes 1769480 | tf_op jit(solution)/shard_map/ppermute | solution.py:41
  298.2 25.6 %collective-permute-start.50 = (bf16[256,1024]{1,0:T(8,128)(2,1)S(1)}, bf16[256,1024]{1,0:T(8,128)(2,1)S(1)}, u32[]{:S(2)}, u32[]{:S(2)}) collective-permute-start(bf16[256,1024]{1,0:T(8,128)(2,1)S(1)} %get-tuple-element.298), channel_id=1, source_target_pairs={{0,1},{1,0},{2,3},{3,2},{4,5},{5,4},{6,7},{7,6},{8,9},{9,8},{10,11... | collective-permute-start | bytes 1572872 | tf_op jit(solution)/shard_map/ppermute | solution.py:41
  298.7 25.0 %collective-permute-start.51 = (bf16[256,1024]{1,0:T(8,128)(2,1)S(1)}, bf16[256,1024]{1,0:T(8,128)(2,1)S(1)}, u32[]{:S(2)}, u32[]{:S(2)}) collective-permute-start(bf16[256,1024]{1,0:T(8,128)(2,1)S(1)} %get-tuple-element.299), channel_id=1, source_target_pairs={{0,2},{1,3},{2,0},{3,1},{4,6},{5,7},{6,4},{7,5},{8,10},{9,11},{10,... | collective-permute-start | bytes 1572872 | tf_op jit(solution)/shard_map/ppermute | solution.py:41
  319.6 14.7 %collective-permute-start.52 = (bf16[256,1024]{1,0:T(8,128)(2,1)S(1)}, bf16[256,1024]{1,0:T(8,128)(2,1)S(1)}, u32[]{:S(2)}, u32[]{:S(2)}) collective-permute-start(bf16[256,1024]{1,0:T(8,128)(2,1)S(1)} %get-tuple-element.300), channel_id=1, source_target_pairs={{0,3},{1,2},{2,1},{3,0},{4,7},{5,6},{6,5},{7,4},{8,11},{9,10},{10,... | collective-permute-start | bytes 1572872 | tf_op jit(solution)/shard_map/ppermute | solution.py:41
  336.3 36.0 %all-to-all-start.2 = ((f32[32,17,128]{2,1,0:T(8,128)}), f32[32,17,128]{2,1,0:T(8,128)S(1)}, u32[]{:S(2)}, u32[]{:S(2)}) async-start(f32[32,17,128]{2,1,0:T(8,128)} %broadcast_in_dim.38), calls=%async_computation.2 | async-start | bytes 786432 | tf_op jit(solution)/shard_map/all_to_all | solution.py:88
  342.1 27.6 %collective-permute-start.57 = (bf16[256,1024]{1,0:T(8,128)(2,1)S(1)}, bf16[256,1024]{1,0:T(8,128)(2,1)}, u32[]{:S(2)}, u32[]{:S(2)}) collective-permute-start(bf16[256,1024]{1,0:T(8,128)(2,1)S(1)} %copy-done.74), channel_id=1, source_target_pairs={{0,3},{1,2},{2,1},{3,0},{4,7},{5,6},{6,5},{7,4},{8,11},{9,10},{10,... | collective-permute-start | bytes 1572872 | tf_op jit(solution)/shard_map/ppermute | solution.py:41
  343.7 23.8 %collective-permute-start.58 = (bf16[384,256]{1,0:T(8,128)(2,1)S(1)}, bf16[384,256]{1,0:T(8,128)(2,1)S(1)}, u32[]{:S(2)}, u32[]{:S(2)}) collective-permute-start(bf16[384,256]{1,0:T(8,128)(2,1)S(1)} %fusion.3), channel_id=1, source_target_pairs={{0,4},{4,0},{1,5},{5,1},{2,6},{6,2},{3,7},{7,3},{8,12},{12,8},{9,1... | collective-permute-start | bytes 589832 | tf_op jit(solution)/shard_map/ppermute | solution.py:41
  (119 other events, 946.3 us)
